TPU v7x, 32 devices: a whole 2x2x4 slice. The times are simulated.
32 devices in a mesh: group: 4 (over y, x), sample: 8 (over z, core).
Axes of the slice: x: 2, y: 2, z: 4, core: 2. Of those that a mesh axis runs over, the one named last changes fastest.
Arguments:
- response_rows: bfloat16 [4096, 4096], P(('group', 'sample')), may hold values from -6 to 6
- prompt_rows: bfloat16 [2048, 4096], P(('group', 'sample')), may hold values from -6 to 6
- queries: bfloat16 [4096, 4096], P(('group', 'sample')), may hold values from -4.5 to 4.5
- response_keys: bfloat16 [4096, 512], P(('group', 'sample')), may hold values from -6 to 6
- prompt_keys: bfloat16 [2048, 512], P(('group', 'sample')), may hold values from -5 to 5
- cotangent: bfloat16 [4096, 4096], P(('group', 'sample')), may hold values from -96 to 96
- segment_index: int32 [32, 128], P(('group', 'sample')), may hold values from 0 to 7, never falling along the last dimension, each value on 1 to 32 neighbouring positions
- prompt_choice: int32 [32, 8], P(('group', 'sample')), may hold values from 0 to 3
- frozen_value_weight: bfloat16 [4096, 512], P('sample'), may hold values from -0.09375 to 0.09375
- value_adapter_down: bfloat16 [4096, 16], P('sample'), may hold values from -0.09375 to 0.09375
- value_adapter_up: bfloat16 [16, 512], replicated, may hold values from -1.5 to 1.5
Outputs:
- response_grad: bfloat16 [4096, 4096], P(('group', 'sample'))
- prompt_grad: bfloat16 [2048, 4096], P(('group', 'sample'))
- response_key_grad: bfloat16 [4096, 512], P(('group', 'sample'))
- prompt_key_grad: bfloat16 [2048, 512], P(('group', 'sample'))
- first_grad: float32 [4096, 16], P('sample')
- second_grad: float32 [16, 512], replicated
Inputs may be any that keep to these rules, and one draw needn't show every extreme that they name: `segment_index`: within the 128 tokens of one device the response number never falls; each of the 8 responses has 1 to 32 tokens, and one has exactly 32.
All inputs are finite; a program needn't handle non-finite values.
Results may differ from a plain program's by a relative error of at most 0.015.
Values may be sent and summed in bfloat16 or wider, within the bound.
A program may use at most 128 MiB of HBM per device.

v0:
```python
import jax
import jax.numpy as jnp
from jax import lax
from jax.sharding import PartitionSpec as P

HEADS = 32
KV_HEADS = 4
HEAD_DIM = 128
PROMPT_LEN = 128


adapter_scale = 2.0


def contract_final_axis(left, right):
    return lax.dot_general(
        left, right, (((1,), (1,)), ((), ())), preferred_element_type=jnp.float32
    )


def contract_first(left, right):
    return lax.dot_general(
        left, right, (((0,), (0,)), ((), ())), preferred_element_type=jnp.float32
    )


def visibility(segments, choices, prompt_total):
    tokens_here = segments.shape[0]
    onehot = (segments[:, None] == jnp.arange(choices.shape[0], dtype=jnp.int32)[None, :]).astype(
        jnp.int32
    )
    token_prompt = jnp.sum(onehot * choices[None, :], axis=1)
    key_prompt = jnp.arange(prompt_total, dtype=jnp.int32) // PROMPT_LEN
    prompt_seen = token_prompt[:, None] == key_prompt[None, :]
    position = jnp.arange(tokens_here, dtype=jnp.int32)
    own_seen = (segments[:, None] == segments[None, :]) & (position[None, :] <= position[:, None])
    return jnp.concatenate([prompt_seen, own_seen], axis=1)


def head_parts(query_rows, cotangent_rows, head_index):
    tokens_here = query_rows.shape[0]
    group_size = HEADS // KV_HEADS
    block_width = group_size * HEAD_DIM
    query_block = query_rows[:, head_index * block_width : (head_index + 1) * block_width].reshape(
        tokens_here, group_size, HEAD_DIM
    )
    cotangent_block = cotangent_rows[
        :, head_index * block_width : (head_index + 1) * block_width
    ].reshape(tokens_here, group_size, HEAD_DIM)
    return (query_block, cotangent_block)


def attend(query_rows, cotangent_rows, key_rows, value_rows, visible):
    score_scale = HEAD_DIM ** (-0.5)
    key_list = []
    value_list = []
    for head_index in range(KV_HEADS):
        query_block, cotangent_block = head_parts(query_rows, cotangent_rows, head_index)
        key_block = key_rows[:, head_index * HEAD_DIM : (head_index + 1) * HEAD_DIM]
        value_block = value_rows[:, head_index * HEAD_DIM : (head_index + 1) * HEAD_DIM]
        scores = (
            jnp.einsum("tgd,sd->gts", query_block, key_block, preferred_element_type=jnp.float32)
            * score_scale
        )
        scores = jnp.where(visible[None], scores, -1e30)
        row_top = jnp.max(scores, axis=-1, keepdims=True)
        powers = jnp.exp(scores - row_top)
        softmax_full = powers / jnp.sum(powers, axis=-1, keepdims=True)
        softmax_low = softmax_full.astype(jnp.bfloat16)
        mixture = jnp.einsum(
            "gts,sd->gtd", softmax_low, value_block, preferred_element_type=jnp.float32
        )
        row_delta = jnp.einsum("tgd,gtd->gt", cotangent_block.astype(jnp.float32), mixture)
        grad_softmax = jnp.einsum(
            "tgd,sd->gts", cotangent_block, value_block, preferred_element_type=jnp.float32
        )
        grad_scores = (softmax_full * (grad_softmax - row_delta[..., None])).astype(jnp.bfloat16)
        key_list.append(
            jnp.einsum("gts,tgd->sd", grad_scores, query_block, preferred_element_type=jnp.float32)
            * score_scale
        )
        value_list.append(
            jnp.einsum(
                "gts,tgd->sd", softmax_low, cotangent_block, preferred_element_type=jnp.float32
            )
        )
    return (jnp.concatenate(key_list, axis=1), jnp.concatenate(value_list, axis=1))


def on_device(
    response_rows,
    prompt_rows,
    queries,
    response_keys,
    prompt_keys,
    cotangent,
    segment_index,
    prompt_choice,
    frozen_value_weight,
    value_adapter_down,
    value_adapter_up,
):
    tokens_here = response_rows.shape[0]
    prompt_here = prompt_rows.shape[0]
    local_rows = jnp.concatenate([response_rows, prompt_rows], axis=0)
    weight_piece = lax.all_gather(frozen_value_weight, "sample", axis=0, tiled=True)
    down_factor_piece = lax.all_gather(value_adapter_down, "sample", axis=0, tiled=True)
    base_run = jnp.dot(local_rows, weight_piece, preferred_element_type=jnp.float32)
    low_run = jnp.dot(local_rows, down_factor_piece, preferred_element_type=jnp.float32)
    down_projection = low_run.astype(jnp.bfloat16)
    value_inputs = (
        base_run
        + adapter_scale
        * jnp.dot(down_projection, value_adapter_up, preferred_element_type=jnp.float32)
    ).astype(jnp.bfloat16)
    key_prefix, value_prefix = (
        lax.all_gather(prompt_keys, "sample", axis=0, tiled=True),
        lax.all_gather(value_inputs[tokens_here:], "sample", axis=0, tiled=True),
    )
    prompt_total = key_prefix.shape[0]
    visible = visibility(segment_index.reshape(-1), prompt_choice.reshape(-1), prompt_total)
    key_rows = jnp.concatenate([key_prefix, response_keys], axis=0)
    value_rows = jnp.concatenate([value_prefix, value_inputs[:tokens_here]], axis=0)
    key_grads, value_grads = attend(queries, cotangent, key_rows, value_rows, visible)
    own_key_grads = key_grads[prompt_total:]
    own_value_grads = value_grads[prompt_total:]
    prompt_key_part, prompt_value_part = (
        lax.psum_scatter(key_grads[:prompt_total], "sample", scatter_dimension=0, tiled=True),
        lax.psum_scatter(value_grads[:prompt_total], "sample", scatter_dimension=0, tiled=True),
    )
    value_low_rank = jnp.concatenate(
        [own_value_grads.astype(jnp.bfloat16), prompt_value_part.astype(jnp.bfloat16)], axis=0
    )
    low_rank_backward = contract_final_axis(value_low_rank, value_adapter_up).astype(jnp.bfloat16)
    adapter_backward = adapter_scale * contract_final_axis(low_rank_backward, down_factor_piece)
    frozen_backward = contract_final_axis(
        value_low_rank, lax.all_gather(frozen_value_weight, "sample", axis=0, tiled=True)
    )
    output_gradient = (frozen_backward + adapter_backward).astype(jnp.bfloat16)
    first_part = contract_first(local_rows, low_rank_backward)
    second_part = contract_first(down_projection, value_low_rank)
    adapter_factor = adapter_scale * float(
        (tokens_here + prompt_here) * lax.axis_size("group") * lax.axis_size("sample")
    ) ** (-0.5)
    slice_rows = value_adapter_down.shape[0]
    first_sum, second_sum = lax.psum((first_part, second_part), ("group", "sample"))
    first_slice = lax.dynamic_slice_in_dim(
        first_sum, lax.axis_index("sample") * slice_rows, slice_rows, 0
    )
    return (
        output_gradient[:tokens_here],
        output_gradient[tokens_here:],
        own_key_grads.astype(jnp.bfloat16),
        prompt_key_part.astype(jnp.bfloat16),
        first_slice * adapter_factor,
        second_sum * adapter_factor,
    )


def solution(mesh):
    in_specs = (
        P(("group", "sample"), None),
        P(("group", "sample"), None),
        P(("group", "sample"), None),
        P(("group", "sample"), None),
        P(("group", "sample"), None),
        P(("group", "sample"), None),
        P(("group", "sample"), None),
        P(("group", "sample"), None),
        P("sample", None),
        P("sample", None),
        P(),
    )
    out_specs = (
        P(("group", "sample"), None),
        P(("group", "sample"), None),
        P(("group", "sample"), None),
        P(("group", "sample"), None),
        P("sample", None),
        P(),
    )
    return jax.shard_map(
        on_device, mesh=mesh, in_specs=in_specs, out_specs=out_specs, check_vma=False
    )
```

profile of v0, /device:TPU:0, one launch (start us, length us, event | category | flops | bytes accessed | tf_op | source)
XLA Modules:
  0.0 309.1 jit_solution(16988363995114479483)
XLA Ops:
  8.8 16.8 %all_gather.13 = bf16[512,512]{1,0:T(8,128)(2,1)S(1)} all-gather(bf16[64,512]{1,0:T(8,128)(2,1)} %param.15), channel_id=1, replica_groups=mesh['group'=4,'sample'=8] {'sample'}, dimensions={0}, use_global_device_ids=true | all-gather | bytes 589824 | tf_op jit(solution)/shard_map/all_gather | solution.py:117
  26.4 1.3 fusion.109
  31.4 1.6 constant_dynamic-update-slice_fusion
  33.0 3.4 %fusion.110 = (f32[8,128]{1,0:T(8,128)S(1)}, f32[8,128,640]{1,2,0:T(8,128)}) fusion(pred[128,640]{0,1:T(8,128)(4,1)S(1)} %pad_add_fusion, bf16[128,8,128]{0,2,1:T(8,128)(2,1)S(1)} %bitcast.234, bf16[640,512]{1,0:T(8,128)(2,1)} %constant_dynamic-update-slice_fusion), kind=kOutput, calls=%fused_computation.154 | convolution fusion | flops 170394240 | bytes 3133440 | tf_op jit(solution)/shard_map/sub | solution.py:67
  36.4 3.3 %fusion.112 = (f32[8,128]{1,0:T(8,128)S(1)}, f32[8,128,640]{1,2,0:T(8,128)}) fusion(pred[128,640]{0,1:T(8,128)(4,1)S(1)} %pad_add_fusion, bf16[128,8,128]{0,2,1:T(8,128)(2,1)S(1)} %bitcast.232, bf16[640,512]{1,0:T(8,128)(2,1)} %constant_dynamic-update-slice_fusion), kind=kOutput, calls=%fused_computation.156 | convolution fusion | flops 170394240 | bytes 3133440 | tf_op jit(solution)/shard_map/sub | solution.py:67
  39.8 2.1 fusion.111
  41.9 3.9 %fusion.113 = (f32[8,128]{1,0:T(8,128)S(1)}, f32[8,128,640]{1,2,0:T(8,128)}) fusion(pred[128,640]{0,1:T(8,128)(4,1)S(1)} %copy-done.28, bf16[128,8,128]{0,2,1:T(8,128)(2,1)} %bitcast.228, bf16[640,512]{1,0:T(8,128)(2,1)} %constant_dynamic-update-slice_fusion), kind=kOutput, calls=%fused_computation.157 | convolution fusion | flops 170394240 | bytes 3133440 | tf_op jit(solution)/shard_map/sub | solution.py:67
  45.8 2.1 fusion.54
  51.1 1.4 copy-done.8
  53.4 1.1 slice.103
  54.5 2.5 copy.161
  57.9 14.1 %all_gather.15 = bf16[4096,16]{0,1:T(8,128)(2,1)S(1)} all-gather(bf16[512,16]{0,1:T(8,128)(2,1)S(1)} %copy-done.31), channel_id=1, replica_groups=mesh['group'=4,'sample'=8] {'sample'}, dimensions={0}, use_global_device_ids=true | all-gather | bytes 147456 | tf_op jit(solution)/shard_map/all_gather | solution.py:107
  72.0 1.3 constant_dynamic-update-slice_fusion.3
  74.4 1.1 convolution_convert_fusion.1
  75.5 15.6 %reduce-scatter.7.cloned.1.call-done = f32[64,512]{1,0:T(8,128)} async-done(((f32[512,512]{1,0:T(8,128)}), f32[64,512]{1,0:T(8,128)}) %reduce-scatter.7.cloned.1.call-update) | async-done | bytes 131088
  94.1 44.0 %all-gather.2.cloned.1.call-done = bf16[4096,512]{1,0:T(8,128)(2,1)} async-done(((bf16[512,512]{1,0:T(8,128)(2,1)}), bf16[4096,512]{1,0:T(8,128)(2,1)}) %all-gather.2.cloned.1.call-update) | async-done | bytes 4194320 | tf_op jit(solution)/shard_map/all_gather | solution.py:137
  138.0 3.3 %fusion.114 = f32[192,512]{1,0:T(8,128)S(1)} fusion(bf16[192,4096]{1,0:T(8,128)(2,1)S(1)} %constant_dynamic-update-slice_fusion.2, bf16[4096,512]{1,0:T(8,128)(2,1)} %all-gather.2.cloned.1.call-done), kind=kOutput, calls=%fused_computation.158 | convolution fusion | flops 805306368 | bytes 6160384 | tf_op jit(solution)/shard_map/dot_general | solution.py:108
  142.3 15.2 %all_gather.16 = bf16[512,512]{1,0:T(8,128)(2,1)S(1)} all-gather(bf16[64,512]{1,0:T(8,128)(2,1)S(1)} %slice.106), channel_id=1, replica_groups=mesh['group'=4,'sample'=8] {'sample'}, dimensions={0}, use_global_device_ids=true | all-gather | bytes 589824 | tf_op jit(solution)/shard_map/all_gather | solution.py:118
  158.1 2.0 fusion.50
  160.1 3.6 %fusion.39 = f32[640,128]{0,1:T(8,128)} fusion(bf16[128,8,128]{0,2,1:T(8,128)(2,1)} %bitcast.235, bf16[640,128,1]{1,0,2:T(8,128)(2,1)} %copy-done.26, bf16[128,8,128]{0,2,1:T(8,128)(2,1)} %bitcast.226, f32[8,128]{1,0:T(8,128)} %fusion.50, f32[8,128,640]{1,2,0:T(8,128)} %get-tuple-element.39, f32[8,128]{1,0:T(8,128)} %copy-done.36), kind=kOutput, calls=%fused_computation.64 | convolution fusion | flops 338247680 | bytes 3645440 | tf_op jit(solution)/shard_map/gts,tgd->sd/dot_general | solution.py:79
  163.7 2.0 fusion.48
  165.7 3.5 %fusion.43 = f32[640,128]{0,1:T(8,128)} fusion(bf16[128,8,128]{0,2,1:T(8,128)(2,1)} %bitcast.233, bf16[128,8,128]{0,2,1:T(8,128)(2,1)} %bitcast.224, f32[8,128]{1,0:T(8,128)} %fusion.48, f32[8,128,640]{1,2,0:T(8,128)} %get-tuple-element.43, f32[8,128]{1,0:T(8,128)} %copy-done.35, bf16[512,512]{1,0:T(8,128)(2,1)S(1)} %all_gather.16, ...), kind=kOutput, calls=%fused_computation.68 | convolution fusion | flops 338575360 | bytes 4136960 | tf_op jit(solution)/shard_map/gts,tgd->sd/dot_general | solution.py:79
  169.2 2.0 fusion.49
  171.1 2.7 fusion.41
  174.3 2.6 fusion.45
  178.3 1.4 copy.163
  179.9 38.5 %psum.15 = f32[16,512]{1,0:T(8,128)S(1)} all-reduce(f32[16,512]{1,0:T(8,128)S(1)} %fusion.74), channel_id=1, replica_groups=mesh['group'=4,'sample'=8] {'group','sample'}, use_global_device_ids=true, to_apply=%region_12.13 | all-reduce | flops 8192 | bytes 65536 | tf_op jit(solution)/shard_map/psum | solution.py:146
  219.0 1.3 convolution_multiply_fusion
  220.3 47.2 %all-reduce.2.cloned.1.call-done = f32[4096,16]{0,1:T(8,128)} async-done(((f32[4096,16]{0,1:T(8,128)}), f32[4096,16]{0,1:T(8,128)}) %all-reduce.2.cloned.1.call-update) | async-done | bytes 262160 | tf_op jit(solution)/shard_map/psum | solution.py:146
  267.5 1.4 dynamic-slice_multiply_fusion
  269.8 3.8 %fusion.4 = bf16[192,4096]{1,0:T(8,128)(2,1)S(1)} fusion(f32[192,4096]{1,0:T(8,128)S(1)} %convolution_multiply_fusion, bf16[4096,512]{1,0:T(8,128)(2,1)} %all-gather.2.cloned.1.call-done, bf16[64,512]{0,1:T(8,128)(2,1)S(1)} %copy-done.20, bf16[128,512]{0,1:T(8,128)(2,1)S(1)} %copy-done.18), kind=kOutput, calls=%fused_computation.6 | convolution fusion | flops 807272448 | bytes 9109504 | tf_op jit(solution)/shard_map/dot_general | solution.py:16
  276.2 24.6 %reduce-scatter.9.cloned.1.call-done = f32[64,512]{1,0:T(8,128)} async-done(((f32[512,512]{1,0:T(8,128)}), f32[64,512]{1,0:T(8,128)}) %reduce-scatter.9.cloned.1.call-update) | async-done | bytes 131088
  (124 shorter events, 24.3 us)
Async XLA Ops:
  7.2 85.0 %copy-start = (bf16[16,512]{1,0:T(8,128)(2,1)S(1)}, bf16[16,512]{1,0:T(8,128)(2,1)}, u32[]{:S(2)}) copy-start(bf16[16,512]{1,0:T(8,128)(2,1)} %param.21) | copy-start | bytes 49156
  7.2 84.0 %reduce-scatter.7.cloned.1.call-start = ((), (), s32[]{:S(2)}) async-start(), calls=%async_computation.4 | async-start | bytes 1179648
  25.6 4.2 %copy-start.15 = (bf16[128,4096]{1,0:T(8,128)(2,1)S(1)}, bf16[128,4096]{1,0:T(8,128)(2,1)}, u32[]{:S(2)}) copy-start(bf16[128,4096]{1,0:T(8,128)(2,1)} %param.16) | copy-start | bytes 3145732
  29.6 6.9 %copy-start.24 = (bf16[128,1024]{0,1:T(8,128)(2,1)}, bf16[128,1024]{0,1:T(8,128)(2,1)S(1)}, u32[]{:S(2)}) copy-start(bf16[128,1024]{0,1:T(8,128)(2,1)S(1)} %copy.166) | copy-start | bytes 786436
  29.7 6.7 %copy-start.25 = (bf16[128,1024]{0,1:T(8,128)(2,1)}, bf16[128,1024]{0,1:T(8,128)(2,1)S(1)}, u32[]{:S(2)}) copy-start(bf16[128,1024]{0,1:T(8,128)(2,1)S(1)} %copy.168) | copy-start | bytes 786436
  30.2 19.0 %copy-start.12 = (bf16[128,1024]{0,1:T(8,128)(2,1)}, bf16[128,1024]{0,1:T(8,128)(2,1)S(1)}, u32[]{:S(2)}) copy-start(bf16[128,1024]{0,1:T(8,128)(2,1)S(1)} %copy.93) | copy-start | bytes 786436
  31.2 19.3 %copy-start.11 = (bf16[128,1024]{0,1:T(8,128)(2,1)}, bf16[128,1024]{0,1:T(8,128)(2,1)S(1)}, u32[]{:S(2)}) copy-start(bf16[128,1024]{0,1:T(8,128)(2,1)S(1)} %copy.97) | copy-start | bytes 786436
  31.4 8.3 %copy-start.27 = (pred[128,640]{0,1:T(8,128)(4,1)}, pred[128,640]{0,1:T(8,128)(4,1)S(1)}, u32[]{:S(2)}) copy-start(pred[128,640]{0,1:T(8,128)(4,1)S(1)} %pad_add_fusion) | copy-start | bytes 245764
  36.4 9.4 %copy-start.36 = (f32[8,128]{1,0:T(8,128)}, f32[8,128]{1,0:T(8,128)S(1)}, u32[]{:S(2)}) copy-start(f32[8,128]{1,0:T(8,128)S(1)} %get-tuple-element.38) | copy-start | bytes 12292
  39.8 9.2 %copy-start.35 = (f32[8,128]{1,0:T(8,128)}, f32[8,128]{1,0:T(8,128)S(1)}, u32[]{:S(2)}) copy-start(f32[8,128]{1,0:T(8,128)S(1)} %get-tuple-element.42) | copy-start | bytes 12292
  39.8 2.1 copy-start.28
  41.8 8.5 %copy-start.9 = (f32[8,128,640]{1,2,0:T(8,128)}, f32[8,128,640]{1,2,0:T(8,128)S(1)}, u32[]{:S(2)}) copy-start(f32[8,128,640]{1,2,0:T(8,128)S(1)} %get-tuple-element.41) | copy-start | bytes 7864324
  41.8 8.5 %copy-start.34 = (f32[8,128]{1,0:T(8,128)}, f32[8,128]{1,0:T(8,128)S(1)}, u32[]{:S(2)}) copy-start(f32[8,128]{1,0:T(8,128)S(1)} %get-tuple-element.40) | copy-start | bytes 12292
  45.8 5.3 %copy-start.32 = (f32[8,128]{1,0:T(8,128)}, f32[8,128]{1,0:T(8,128)S(1)}, u32[]{:S(2)}) copy-start(f32[8,128]{1,0:T(8,128)S(1)} %get-tuple-element.44) | copy-start | bytes 12292
  45.8 2.1 copy-start.16
  45.8 3.2 %copy-start.10 = (f32[8,128,640]{1,2,0:T(8,128)S(1)}, f32[8,128,640]{1,2,0:T(8,128)}, u32[]{:S(2)}) copy-start(f32[8,128,640]{1,2,0:T(8,128)} %get-tuple-element.43) | copy-start | bytes 7864324
  50.3 2.2 copy-start.8
  50.5 2.2 copy-start.1
  53.4 4.5 %copy-start.31 = (bf16[512,16]{0,1:T(8,128)(2,1)S(1)}, bf16[512,16]{0,1:T(8,128)(2,1)}, u32[]{:S(2)}) copy-start(bf16[512,16]{0,1:T(8,128)(2,1)} %param.20) | copy-start | bytes 49156
  57.1 80.9 %all-gather.2.cloned.1.call-start = ((), (), s32[]{:S(2)}) async-start(), calls=%async_computation.2 | async-start | bytes 4718592 | tf_op jit(solution)/shard_map/all_gather | solution.py:137
  57.8 209.6 %all-reduce.2.cloned.1.call-start = ((), (), s32[]{:S(2)}) async-start(), calls=%async_computation.3 | async-start | bytes 524288 | tf_op jit(solution)/shard_map/psum | solution.py:146
  57.9 34.3 %copy-start.17 = (bf16[128,512]{0,1:T(8,128)(2,1)}, bf16[128,512]{0,1:T(8,128)(2,1)S(1)}, u32[]{:S(2)}) copy-start(bf16[128,512]{0,1:T(8,128)(2,1)S(1)} %slice.185) | copy-start | bytes 393220
  72.0 20.4 %copy-start.13 = (bf16[4096,16]{0,1:T(8,128)(2,1)}, bf16[4096,16]{0,1:T(8,128)(2,1)S(1)}, u32[]{:S(2)}) copy-start(bf16[4096,16]{0,1:T(8,128)(2,1)S(1)} %all_gather.15) | copy-start | bytes 393220
  94.0 206.8 %reduce-scatter.9.cloned.1.call-start = ((), (), s32[]{:S(2)}) async-start(), calls=%async_computation.5 | async-start | bytes 1179648
  138.0 20.1 %copy-start.6 = (bf16[8,128,640]{1,2,0:T(8,128)(2,1)S(1)}, bf16[8,128,640]{1,2,0:T(8,128)(2,1)}, u32[]{:S(2)}) copy-start(bf16[8,128,640]{1,2,0:T(8,128)(2,1)} %copy-done.5) | copy-start | bytes 3932164
  160.1 3.6 %copy-start.4 = (bf16[8,128,640]{1,2,0:T(8,128)(2,1)S(1)}, bf16[8,128,640]{1,2,0:T(8,128)(2,1)}, u32[]{:S(2)}) copy-start(bf16[8,128,640]{1,2,0:T(8,128)(2,1)} %copy-done.3) | copy-start | bytes 3932164
  165.6 3.5 %copy-start.2 = (bf16[8,128,640]{1,2,0:T(8,128)(2,1)S(1)}, bf16[8,128,640]{1,2,0:T(8,128)(2,1)}, u32[]{:S(2)}) copy-start(bf16[8,128,640]{1,2,0:T(8,128)(2,1)} %copy-done.1) | copy-start | bytes 3932164
  171.1 3.2 %copy-start.23 = (bf16[128,1024]{0,1:T(8,128)(2,1)S(1)}, bf16[128,1024]{0,1:T(8,128)(2,1)}, u32[]{:S(2)}) copy-start(bf16[128,1024]{0,1:T(8,128)(2,1)} %copy.165) | copy-start | bytes 786436
  171.1 3.2 %copy-start.33 = (f32[8,128]{1,0:T(8,128)S(1)}, f32[8,128]{1,0:T(8,128)}, u32[]{:S(2)}) copy-start(f32[8,128]{1,0:T(8,128)} %copy-done.32) | copy-start | bytes 12292
  174.3 2.7 copy-start.21
  174.3 2.7 copy-start.22
  178.2 40.8 %copy-start.14 = (bf16[4096,16]{0,1:T(8,128)(2,1)S(1)}, bf16[4096,16]{0,1:T(8,128)(2,1)}, u32[]{:S(2)}) copy-start(bf16[4096,16]{0,1:T(8,128)(2,1)} %copy-done.13) | copy-start | bytes 393220
  (9 other events, 11.0 us)
Sparse Core Ops, SparseCore 0:
  57.2 33.8 reduce-scatter.6
  92.7 45.2 all-gather.1
  143.5 123.8 all-reduce.1
  269.6 31.1 reduce-scatter.8
where the time goes:
time: 310 us; the launch traced here: 309 us
  waiting for transfers between devices  132 us (43%)
  blocking collectives  84.5 us (27%)
  matrix products  45.3 us (15%)
  local copies, waits for them, and re-layouts  26.1 us (8%)
  between operations  14.3 us (5%)
  other arithmetic  6.68 us (2%)
    psum x1, waiting for transfers between devices, on_device(): lax.psum((first_part, second_part), ('group', 'sample'))  47.2 us
    all_gather x1, waiting for transfers between devices, on_device(): lax.all_gather(frozen_value_weight, 'sample', axis=0, tiled=True)  44 us
    unnamed x6, waiting for transfers between devices  40.9 us
    psum x1, blocking collectives, on_device(): lax.psum((first_part, second_part), ('group', 'sample'))  38.5 us
    all_gather x1, blocking collectives, on_device(): lax.all_gather(prompt_keys, 'sample', axis=0, tiled=True)  16.8 us
    unnamed x86, local copies, waits for them, and re-layouts  16.5 us
    all_gather x1, blocking collectives, on_device(): lax.all_gather(value_inputs[tokens_here:], 'sample', axis=0, tiled=True)  15.2 us
    all_gather x1, blocking collectives, on_device(): lax.all_gather(value_adapter_down, 'sample', axis=0, tiled=True)  14.1 us
  transfers between devices with their start and end apart: 4, of which 4 were waited for; matrix products, arithmetic and copies ran while one was open for 13% of the time, Pallas kernels for 0%

commit v1 on v0

v1 whole, which is shorter than its diff:
```python
import functools

import jax
import jax.numpy as jnp
from jax import lax
from jax.experimental import pallas as pl
from jax.experimental.pallas import tpu as pltpu
from jax.sharding import PartitionSpec as P

HEADS = 32
KV_HEADS = 4
HEAD_DIM = 128
PROMPT_LEN = 128
GROUP_SIZE = HEADS // KV_HEADS
SCORE_SCALE = HEAD_DIM ** (-0.5)

adapter_scale = 2.0

BF = jnp.bfloat16
F32 = jnp.float32
MESH = pl.DeviceIdType.MESH


def nt(left, right):
    return lax.dot_general(left, right, (((1,), (1,)), ((), ())), preferred_element_type=F32)


def tn(left, right):
    return lax.dot_general(left, right, (((0,), (0,)), ((), ())), preferred_element_type=F32)


def nn(left, right):
    return lax.dot_general(left, right, (((1,), (0,)), ((), ())), preferred_element_type=F32)


class Slots:
    def __init__(self):
        self.count = 0

    def take(self, number):
        base = self.count
        self.count += number
        return base


def layout(nz, n_group):
    slots = Slots()
    places = {name: slots.take(nz) for name in (
        "k_z", "k_c", "d_z", "d_c", "v_z", "v_c",
        "w_z", "w_c", "w_x", "w_y", "w_d0", "w_d1",
        "rv_z", "rk_z", "ra_z",
    )}
    for name in ("rv_c", "rk_c", "ra_c"):
        places[name] = slots.take(1)
    places["g"] = slots.take(n_group)
    places["local"] = slots.take(4)
    return places, slots.count


def kernel(
    nz, n_group, places, factor,
    xr, xp, q, ct, w, rk, pk, seg, ch, dn, up,
    o_rg, o_pg, o_rk, o_pk, o_f, o_s,
    xv, qv, cv, wfull, kall, vall, dall, pmask, obias, prob, vlow, vloc, vp, acc, low,
    gv, gv_p, gv_h, gv_r, gk, gk_p, gk_h, gk_r, ga, ga_p, ga_h, ga_r, gg,
    ssem, rsem,
):
    g = lax.axis_index("group")
    j = lax.axis_index("sample")
    z = j // 2
    c = j % 2
    oc = 1 - c
    tokens = q.shape[0]
    rows = pk.shape[0]
    shard = w.shape[0]
    quarter = shard // 4
    half = quarter // 2
    prompts = 2 * nz * rows // PROMPT_LEN
    nzp = PROMPT_LEN // rows // 2
    partner = (g, j + 1 - 2 * c)
    gx = g + 1 - 2 * (g % 2)
    gy = g + 2 - 4 * ((g // 2) % 2)
    qme, qx, qy = g % 4, gx % 4, gy % 4
    qd = 3 - qme

    def zat(dz):
        return lax.rem(z + dz, nz)

    def zdev(dz):
        return (g, 2 * zat(dz) + c)

    def rcopy(src, dst, name, send, recv, device):
        return pltpu.make_async_remote_copy(
            src_ref=src, dst_ref=dst,
            send_sem=ssem.at[places[name] + send], recv_sem=rsem.at[places[name] + recv],
            device_id=device, device_id_type=MESH,
        )

    sends = []

    def go(copy):
        copy.start()
        sends.append(copy)

    def gather_start(src, buf, name_z, name_c):
        for dz in range(1, nz):
            go(rcopy(src, buf.at[z, c], name_z, dz, nz - dz, zdev(dz)))
        go(rcopy(src, buf.at[z, c], name_c, 0, 0, partner))

    def gather_forward(buf, name_z, name_c):
        for dz in range(1, nz):
            there = buf.at[zat(dz), c]
            rcopy(there, there, name_z, dz, dz, zdev(dz)).wait_recv()
            go(rcopy(there, there, name_c, dz, dz, partner))

    def gather_finish(buf, name_c):
        for dz in range(nz):
            there = buf.at[zat(dz), oc]
            rcopy(there, there, name_c, dz, dz, partner).wait_recv()

    def scatter_pair(part, pair, name_c):
        go(rcopy(part.at[:, oc], pair, name_c, 0, 0, partner))

    def scatter_z(part, pair, held, slots, name_c, name_z):
        rcopy(part.at[:, oc], pair, name_c, 0, 0, partner).wait_recv()
        held[...] = (part[:, c].astype(F32) + pair[...].astype(F32)).astype(BF)
        for dz in range(1, nz):
            go(rcopy(held.at[zat(dz)], slots.at[z], name_z, dz, nz - dz, zdev(dz)))
        slots[z] = held[z]

    def scatter_sum(slots, name_z):
        for dz in range(1, nz):
            there = slots.at[zat(dz)]
            rcopy(there, there, name_z, dz, dz, zdev(dz)).wait_recv()
        total = slots[0].astype(F32)
        for at in range(1, nz):
            total = total + slots[at].astype(F32)
        return total

    local = [
        pltpu.make_async_copy(src, dst, ssem.at[places["local"] + at])
        for at, (src, dst) in enumerate((
            (q, qv), (ct, cv), (xr, xv.at[pl.ds(0, tokens)]), (xp, xv.at[pl.ds(tokens, rows)])))
    ]
    for copy in local:
        copy.start()

    barrier = pltpu.get_barrier_semaphore()
    for dz in range(1, nz):
        pl.semaphore_signal(barrier, inc=1, device_id=zdev(dz), device_id_type=MESH)
    pl.semaphore_signal(barrier, inc=1, device_id=partner, device_id_type=MESH)
    for dg in range(1, n_group):
        pl.semaphore_signal(barrier, inc=1, device_id=(lax.rem(g + dg, n_group), j), device_id_type=MESH)
    pl.semaphore_wait(barrier, nz + n_group - 1)

    gather_start(pk, kall, "k_z", "k_c")
    mine = pl.ds(pl.multiple_of(qme * quarter, 16), quarter)
    for dz in range(1, nz):
        go(rcopy(w.at[mine], wfull.at[z, c, mine], "w_z", dz, nz - dz, zdev(dz)))
    go(rcopy(w, wfull.at[z, c], "w_c", 0, 0, partner))
    own_w = pltpu.make_async_copy(w, wfull.at[z, c], ssem.at[places["w_z"]])
    own_w.start()

    dall[z, c] = dn[...]
    gather_start(dn, dall, "d_z", "d_c")
    kall[z, c] = pk[...]

    seg_row = jnp.broadcast_to(seg[...], (tokens, tokens)).astype(F32)
    seg_col = jnp.transpose(seg_row)
    token = lax.broadcasted_iota(jnp.int32, (tokens, tokens), 0)
    other = lax.broadcasted_iota(jnp.int32, (tokens, tokens), 1)
    obias[...] = jnp.where((seg_row == seg_col) & (other <= token), 0.0, -1e30)
    choice = jnp.zeros((tokens, tokens), jnp.int32)
    for at in range(ch.shape[1]):
        choice = jnp.where(seg_col == float(at), ch[0, at], choice)
    for at in range(prompts):
        pmask[at] = jnp.where(choice == at, 1.0, 0.0).astype(BF)

    gather_forward(kall, "k_z", "k_c")
    local[0].wait()
    local[1].wait()
    gather_finish(kall, "k_c")

    def stack(ref, head):
        return [ref[:, pl.ds(pl.multiple_of((head * GROUP_SIZE + at) * HEAD_DIM, HEAD_DIM), HEAD_DIM)]
                for at in range(GROUP_SIZE)]

    def masked(parts):
        return jnp.concatenate(
            [jnp.concatenate([part * pmask[at] for part in parts], axis=0) for at in range(prompts)], axis=1)

    def side(buf, lanes):
        return jnp.concatenate(
            [buf[at * nzp:(at + 1) * nzp, :, :, lanes].reshape(PROMPT_LEN, HEAD_DIM) for at in range(prompts)],
            axis=1)

    def head_lanes(head):
        return pl.ds(pl.multiple_of(head * HEAD_DIM, HEAD_DIM), HEAD_DIM)

    def spread(buf, lanes, block):
        for at in range(prompts):
            buf[at * nzp:(at + 1) * nzp, :, :, lanes] = block[
                :, at * HEAD_DIM:(at + 1) * HEAD_DIM].astype(BF).reshape(nzp, 2, rows, HEAD_DIM)

    def softmax_head(head, carry):
        lanes = head_lanes(head)
        qs = stack(qv, head)
        s_sel = nt(masked(qs), side(kall, lanes)) * SCORE_SCALE
        s_own = nt(jnp.concatenate(qs, axis=0), rk[:, lanes]) * SCORE_SCALE
        s_own = s_own + jnp.concatenate([obias[...]] * GROUP_SIZE, axis=0)
        top = jnp.max(jnp.maximum(s_sel, s_own), axis=-1, keepdims=True)
        e_sel = jnp.exp(s_sel - top)
        e_own = jnp.exp(s_own - top)
        inv = 1.0 / jnp.sum(e_sel + e_own, axis=-1, keepdims=True)
        p_sel = e_sel * inv
        p_own = e_own * inv
        prob[head, :, 0:PROMPT_LEN] = p_sel
        prob[head, :, PROMPT_LEN:] = p_own
        cs = stack(cv, head)
        spread(gv, lanes, tn(p_sel.astype(BF), masked(cs)))
        vlow[0:tokens, lanes] = tn(p_own.astype(BF), jnp.concatenate(cs, axis=0)).astype(BF)
        return carry

    def w_plane(dz):
        there = wfull.at[zat(dz), c, mine]
        rcopy(there, there, "w_z", dz, dz, zdev(dz)).wait_recv()
        go(rcopy(there, there, "w_x", dz, dz, (gx, j)))
        go(rcopy(there, there, "w_y", dz, dz, (gy, j)))

    def w_diagonal(dz):
        at_x = pl.ds(pl.multiple_of(qx * quarter, 16), quarter)
        at_y = pl.ds(pl.multiple_of(qy * quarter, 16), quarter)
        there = wfull.at[zat(dz), c, at_x]
        rcopy(there, there, "w_x", dz, dz, (gx, j)).wait_recv()
        first = wfull.at[zat(dz), c, pl.ds(pl.multiple_of(qx * quarter, 16), half)]
        go(rcopy(first, first, "w_d0", dz, dz, (gy, j)))
        there = wfull.at[zat(dz), c, at_y]
        rcopy(there, there, "w_y", dz, dz, (gy, j)).wait_recv()
        second = wfull.at[zat(dz), c, pl.ds(pl.multiple_of(qy * quarter + half, 16), half)]
        go(rcopy(second, second, "w_d1", dz, dz, (gx, j)))

    def w_chip(dz):
        first = wfull.at[zat(dz), c, pl.ds(pl.multiple_of(qd * quarter, 16), half)]
        rcopy(first, first, "w_d0", dz, dz, (gy, j)).wait_recv()
        second = wfull.at[zat(dz), c, pl.ds(pl.multiple_of(qd * quarter + half, 16), half)]
        rcopy(second, second, "w_d1", dz, dz, (gx, j)).wait_recv()
        there = wfull.at[zat(dz), c]
        go(rcopy(there, there, "w_c", dz, dz, partner))

    lax.fori_loop(0, KV_HEADS // 2, softmax_head, 0)
    for dz in range(1, nz):
        w_plane(dz)
    lax.fori_loop(KV_HEADS // 2, KV_HEADS, softmax_head, 0)
    scatter_pair(gv, gv_p, "rv_c")
    for dz in range(1, nz):
        w_diagonal(dz)
    gather_forward(dall, "d_z", "d_c")
    scatter_z(gv, gv_p, gv_h, gv_r, "rv_c", "rv_z")
    local[2].wait()
    local[3].wait()
    own_w.wait()
    gather_finish(dall, "d_c")

    def columns(z_at, c_at):
        return pl.ds(pl.multiple_of((2 * z_at + c_at) * shard, 128), shard)

    def forward(z_at, c_at, first):
        x = xv[:, columns(z_at, c_at)]
        base = nn(x, wfull[z_at, c_at])
        lowest = nt(x, dall[z_at, c_at])
        acc[...] = base if first else acc[...] + base
        low[...] = lowest if first else low[...] + lowest

    forward(z, c, True)
    for dz in range(1, nz):
        w_chip(dz)
        forward(zat(dz), c, False)
    for dz in range(nz):
        there = wfull.at[zat(dz), oc]
        rcopy(there, there, "w_c", dz, dz, partner).wait_recv()
        forward(zat(dz), oc, False)
    first_proj = low[...].astype(BF)
    values = (acc[...] + adapter_scale * nn(first_proj, up[...])).astype(BF)
    vp[...] = values[tokens:]
    vloc[...] = values[:tokens]
    vall[z, c] = values[tokens:]
    gather_start(vp, vall, "v_z", "v_c")

    def back(first_row, count, out):
        rows_here = vlow[first_row:first_row + count]
        back_low = nt(rows_here, up[...]).astype(BF)

        def one(at, carry):
            z_at, c_at = at // 2, at % 2
            out[:, columns(z_at, c_at)] = (
                nt(rows_here, wfull[z_at, c_at]) + adapter_scale * nn(back_low, dall[z_at, c_at])).astype(BF)
            return carry

        lax.fori_loop(0, 2 * nz, one, 0)

    back(0, tokens, o_rg)
    vlow[tokens:] = scatter_sum(gv_r, "rv_z").astype(BF)
    back_all = nt(vlow[...], up[...]).astype(BF)
    second = tn(first_proj, vlow[...]).astype(BF)

    def adapter(at, carry):
        z_at, c_at = at // 2, at % 2
        ga[z_at, c_at, :, 0:shard] = tn(back_all, xv[:, columns(z_at, c_at)]).astype(BF)
        ga[z_at, c_at, :, shard:] = second
        return carry

    lax.fori_loop(0, 2 * nz, adapter, 0)
    scatter_pair(ga, ga_p, "ra_c")
    back(tokens, rows, o_pg)
    gather_forward(vall, "v_z", "v_c")
    scatter_z(ga, ga_p, ga_h, ga_r, "ra_c", "ra_z")
    gather_finish(vall, "v_c")

    def key_head(head, carry):
        lanes = head_lanes(head)
        cs = stack(cv, head)
        d_sel = nt(masked(cs), side(vall, lanes))
        d_own = nt(jnp.concatenate(cs, axis=0), vloc[:, lanes])
        p_sel = prob[head, :, 0:PROMPT_LEN]
        p_own = prob[head, :, PROMPT_LEN:]
        delta = jnp.sum(p_sel.astype(BF).astype(F32) * d_sel + p_own.astype(BF).astype(F32) * d_own,
                        axis=-1, keepdims=True)
        g_sel = (p_sel * (d_sel - delta)).astype(BF)
        g_own = (p_own * (d_own - delta)).astype(BF)
        qs = stack(qv, head)
        spread(gk, lanes, tn(g_sel, masked(qs)) * SCORE_SCALE)
        o_rk[:, lanes] = (tn(g_own, jnp.concatenate(qs, axis=0)) * SCORE_SCALE).astype(BF)
        return carry

    lax.fori_loop(0, KV_HEADS, key_head, 0)
    scatter_pair(gk, gk_p, "rk_c")
    gg[g] = scatter_sum(ga_r, "ra_z").astype(BF)
    for dg in range(1, n_group):
        there = lax.rem(g + dg, n_group)
        go(rcopy(gg.at[g], gg.at[g], "g", dg, n_group - dg, (there, j)))
    scatter_z(gk, gk_p, gk_h, gk_r, "rk_c", "rk_z")
    for dg in range(1, n_group):
        there = lax.rem(g + dg, n_group)
        rcopy(gg.at[there], gg.at[there], "g", dg, dg, (there, j)).wait_recv()
    total = gg[0].astype(F32)
    for at in range(1, n_group):
        total = total + gg[at].astype(F32)
    total = total * factor
    o_f[...] = total[:, 0:shard]
    o_s[...] = total[:, shard:]
    o_pk[...] = scatter_sum(gk_r, "rk_z").astype(BF)
    for copy in sends:
        copy.wait_send()


def on_device(
    n_group, n_sample,
    response_rows, prompt_rows, queries, response_keys, prompt_keys, cotangent,
    segment_index, prompt_choice, frozen_value_weight, value_adapter_down, value_adapter_up,
):
    tokens, d = response_rows.shape
    rows, kv = prompt_keys.shape
    shard, rank = value_adapter_down.shape
    nz = n_sample // 2
    places, count = layout(nz, n_group)
    factor = adapter_scale * float((tokens + rows) * n_group * n_sample) ** (-0.5)
    wide = shard + kv
    any_space = pl.BlockSpec(memory_space=pl.ANY)
    vmem = pl.BlockSpec(memory_space=pltpu.VMEM)
    smem = pl.BlockSpec(memory_space=pltpu.SMEM)

    def reduce_space(high, across):
        return [
            pltpu.VMEM((nz, 2, high, across), BF),
            pltpu.VMEM((nz, high, across), BF),
            pltpu.VMEM((nz, high, across), BF),
            pltpu.VMEM((nz, high, across), BF),
        ]

    outs = pl.pallas_call(
        functools.partial(kernel, nz, n_group, places, factor),
        out_shape=(
            jax.ShapeDtypeStruct((tokens, d), BF),
            jax.ShapeDtypeStruct((rows, d), BF),
            jax.ShapeDtypeStruct((tokens, kv), BF),
            jax.ShapeDtypeStruct((rows, kv), BF),
            jax.ShapeDtypeStruct((rank, shard), F32),
            jax.ShapeDtypeStruct((rank, kv), F32),
        ),
        in_specs=[any_space] * 5 + [vmem] * 3 + [smem] + [vmem] * 2,
        out_specs=(vmem,) * 6,
        scratch_shapes=[
            pltpu.VMEM((tokens + rows, d), BF),
            pltpu.VMEM((tokens, HEADS * HEAD_DIM), BF),
            pltpu.VMEM((tokens, HEADS * HEAD_DIM), BF),
            pltpu.VMEM((nz, 2, shard, kv), BF),
            pltpu.VMEM((nz, 2, rows, kv), BF),
            pltpu.VMEM((nz, 2, rows, kv), BF),
            pltpu.VMEM((nz, 2, rank, shard), BF),
            pltpu.VMEM((n_sample * rows // PROMPT_LEN, tokens, HEAD_DIM), BF),
            pltpu.VMEM((tokens, tokens), F32),
            pltpu.VMEM((KV_HEADS, GROUP_SIZE * tokens, PROMPT_LEN + tokens), F32),
            pltpu.VMEM((tokens + rows, kv), BF),
            pltpu.VMEM((tokens, kv), BF),
            pltpu.VMEM((rows, kv), BF),
            pltpu.VMEM((tokens + rows, kv), F32),
            pltpu.VMEM((tokens + rows, rank), F32),
            *reduce_space(rows, kv),
            *reduce_space(rows, kv),
            *reduce_space(rank, wide),
            pltpu.VMEM((n_group, rank, wide), BF),
            pltpu.SemaphoreType.DMA((count,)),
            pltpu.SemaphoreType.DMA((count,)),
        ],
        compiler_params=pltpu.CompilerParams(
            collective_id=0, has_side_effects=True, vmem_limit_bytes=56 * 1024 * 1024
        ),
        name="value_backward",
    )(
        response_rows, prompt_rows, queries, cotangent, frozen_value_weight,
        response_keys, prompt_keys, segment_index, prompt_choice, value_adapter_down.T, value_adapter_up,
    )
    return (*outs[:4], outs[4].T, outs[5])


def solution(mesh):
    both = P(("group", "sample"), None)
    in_specs = (both,) * 8 + (P("sample", None), P("sample", None), P())
    out_specs = (both,) * 4 + (P("sample", None), P())
    return jax.shard_map(
        functools.partial(on_device, mesh.shape["group"], mesh.shape["sample"]),
        mesh=mesh, in_specs=in_specs, out_specs=out_specs, check_vma=False,
    )
```

time: 310 us -> 71.3 us (0.23)
  waiting for transfers between devices: 132 us -> 0 us
  blocking collectives: 84.5 us -> 0 us
  Pallas kernels: 0 us -> 63.9 us
  matrix products: 45.3 us -> 0 us
  local copies, waits for them, and re-layouts: 26.1 us -> 6.37 us
  between operations: 14.3 us -> 0.66 us
  other arithmetic: 6.68 us -> 0 us
    pallas_call x0 -> x1, Pallas kernels: none -> 63.9 us  [on_device(): pl.pallas_call(functools.partial(kernel, nz, n_group, places, factor), ou...]
    psum x1 -> x0, waiting for transfers between devices: 47.2 us -> none  [on_device(): lax.psum((first_part, second_part), ('group', 'sample'))]
    all_gather x3 -> x0, blocking collectives: 46 us -> none  [the longest x1 16.8 us: on_device(): lax.all_gather(prompt_keys, 'sample', axis=0, tiled=True)]
    all_gather x1 -> x0, waiting for transfers between devices: 44 us -> none  [on_device(): lax.all_gather(frozen_value_weight, 'sample', axis=0, tiled=True)]
    unnamed x6 -> x0, waiting for transfers between devices: 40.9 us -> none
    psum x1 -> x0, blocking collectives: 38.5 us -> none  [on_device(): lax.psum((first_part, second_part), ('group', 'sample'))]
    dot_general x16 -> x0, matrix products: 26.2 us -> none  [the longest x4 12.4 us: attend(): jnp.einsum('gts,tgd->sd', grad_scores, query_block, preferred_element_typ...]
    sub x4 -> x0, matrix products: 12.7 us -> none  [attend(): powers = jnp.exp(scores - row_top)]
  transfers between devices with their start and end apart: 4 -> 0, of which waited for: 4 -> 0; matrix products, arithmetic and copies ran while one was open for 13% -> 0% of each run, Pallas kernels for 0% -> 0%
where the time goes in v1:
time: 71.3 us; the launch traced here: 71 us
  Pallas kernels  63.9 us (90%)
  local copies, waits for them, and re-layouts  6.37 us (9%)
    pallas_call x1, Pallas kernels, on_device(): pl.pallas_call(functools.partial(kernel, nz, n_group, places, factor), ou...  63.9 us
    unnamed x16, local copies, waits for them, and re-layouts  6.37 us

profile of v1, /device:TPU:0, one launch (start us, length us, event | category | flops | bytes accessed | tf_op | source)
XLA Modules:
  0.0 71.0 jit_solution(13216385843148759806)
XLA Ops:
  0.6 63.9 %value_backward.1 = (bf16[128,4096]{1,0:T(8,128)(2,1)}, bf16[64,4096]{1,0:T(8,128)(2,1)}, bf16[128,512]{1,0:T(8,128)(2,1)}, bf16[64,512]{1,0:T(8,128)(2,1)}, f32[16,512]{1,0:T(8,128)}, /*index=5*/f32[16,512]{1,0:T(8,128)}) custom-call(bf16[128,4096]{1,0:T(8,128)(2,1)} %xr.1, bf16[64,4096]{1,0:T(8,128)(2,1)} %xp.1, bf16[128,4096]{1,0:T(8,128)(2,1)} %q.1, ...), custom_call_target="tpu_custom_call" | custom-call | tf_op jit(solution)/shard_map/value_backward/pallas_call | solution.py:380
  64.6 0.0 copy-start
  64.6 2.3 %copy.23 = bf16[128,4096]{1,0:T(8,128)(2,1)} copy(bf16[128,4096]{1,0:T(8,128)(2,1)} %get-tuple-element.24) | data formatting | bytes 2097152
  66.9 0.0 copy-done
  66.9 0.0 copy-start.1
  66.9 0.8 %copy.24 = bf16[64,4096]{1,0:T(8,128)(2,1)} copy(bf16[64,4096]{1,0:T(8,128)(2,1)S(1)} %copy-done) | data formatting | bytes 1048576
  67.7 0.2 copy-done.1
  68.0 0.0 copy-start.2
  68.0 0.7 copy.25
  68.6 0.2 copy-done.2
  68.8 0.0 copy-start.4
  68.8 0.6 copy.26
  69.4 0.1 copy-done.4
  69.6 0.0 copy-start.3
  69.6 0.6 copy.27
  70.2 0.2 copy-done.3
  70.3 0.6 copy.28
Async XLA Ops:
  64.6 2.4 %copy-start = (bf16[64,4096]{1,0:T(8,128)(2,1)S(1)}, bf16[64,4096]{1,0:T(8,128)(2,1)}, u32[]{:S(2)}) copy-start(bf16[64,4096]{1,0:T(8,128)(2,1)} %get-tuple-element.25) | copy-start | bytes 1572868
  66.9 1.0 %copy-start.1 = (bf16[128,512]{1,0:T(8,128)(2,1)S(1)}, bf16[128,512]{1,0:T(8,128)(2,1)}, u32[]{:S(2)}) copy-start(bf16[128,512]{1,0:T(8,128)(2,1)} %get-tuple-element.26) | copy-start | bytes 393220
  68.0 0.9 %copy-start.2 = (bf16[64,512]{1,0:T(8,128)(2,1)S(1)}, bf16[64,512]{1,0:T(8,128)(2,1)}, u32[]{:S(2)}) copy-start(bf16[64,512]{1,0:T(8,128)(2,1)} %get-tuple-element.27) | copy-start | bytes 196612
  68.8 0.8 %copy-start.4 = (f32[16,512]{1,0:T(8,128)S(1)}, f32[16,512]{1,0:T(8,128)}, u32[]{:S(2)}) copy-start(f32[16,512]{1,0:T(8,128)} %get-tuple-element.16) | copy-start | bytes 98308
  69.6 0.8 %copy-start.3 = (f32[16,512]{1,0:T(8,128)S(1)}, f32[16,512]{1,0:T(8,128)}, u32[]{:S(2)}) copy-start(f32[16,512]{1,0:T(8,128)} %get-tuple-element.29) | copy-start | bytes 98308

commit v2 on v1

--- a/solution.py
+++ b/solution.py
@@ -48,9 +48,9 @@
     places = {name: slots.take(nz) for name in (
         "k_z", "k_c", "d_z", "d_c", "v_z", "v_c",
         "w_z", "w_c", "w_x", "w_y", "w_d0", "w_d1",
-        "rv_z", "rk_z", "ra_z",
+        "rv_z", "rk_z", "rk_z2", "ra_z",
     )}
-    for name in ("rv_c", "rk_c", "ra_c"):
+    for name in ("rv_c", "rk_c", "rk_c2", "ra_c"):
         places[name] = slots.take(1)
     places["g"] = slots.take(n_group)
     places["local"] = slots.take(4)
@@ -96,6 +96,8 @@
             device_id=device, device_id_type=MESH,
         )
 
+    near = [dz for dz in range(1, nz) if dz in (1, nz - 1)]
+    far = [dz for dz in range(1, nz) if dz not in near]
     sends = []
 
     def go(copy):
@@ -155,7 +157,7 @@
 
     gather_start(pk, kall, "k_z", "k_c")
     mine = pl.ds(pl.multiple_of(qme * quarter, 16), quarter)
-    for dz in range(1, nz):
+    for dz in near + far:
         go(rcopy(w.at[mine], wfull.at[z, c, mine], "w_z", dz, nz - dz, zdev(dz)))
     go(rcopy(w, wfull.at[z, c], "w_c", 0, 0, partner))
     own_w = pltpu.make_async_copy(w, wfull.at[z, c], ssem.at[places["w_z"]])
@@ -169,7 +171,7 @@
     seg_col = jnp.transpose(seg_row)
     token = lax.broadcasted_iota(jnp.int32, (tokens, tokens), 0)
     other = lax.broadcasted_iota(jnp.int32, (tokens, tokens), 1)
-    obias[...] = jnp.where((seg_row == seg_col) & (other <= token), 0.0, -1e30)
+    obias[...] = jnp.where((seg_row == seg_col) & (token <= other), 0.0, -1e30)
     choice = jnp.zeros((tokens, tokens), jnp.int32)
     for at in range(ch.shape[1]):
         choice = jnp.where(seg_col == float(at), ch[0, at], choice)
@@ -202,24 +204,23 @@
             buf[at * nzp:(at + 1) * nzp, :, :, lanes] = block[
                 :, at * HEAD_DIM:(at + 1) * HEAD_DIM].astype(BF).reshape(nzp, 2, rows, HEAD_DIM)
 
-    def softmax_head(head, carry):
+    def softmax_head(head):
         lanes = head_lanes(head)
         qs = stack(qv, head)
-        s_sel = nt(masked(qs), side(kall, lanes)) * SCORE_SCALE
-        s_own = nt(jnp.concatenate(qs, axis=0), rk[:, lanes]) * SCORE_SCALE
-        s_own = s_own + jnp.concatenate([obias[...]] * GROUP_SIZE, axis=0)
-        top = jnp.max(jnp.maximum(s_sel, s_own), axis=-1, keepdims=True)
+        s_sel = nt(side(kall, lanes), masked(qs)) * SCORE_SCALE
+        s_own = nt(rk[:, lanes], jnp.concatenate(qs, axis=0)) * SCORE_SCALE
+        s_own = s_own + jnp.concatenate([obias[...]] * GROUP_SIZE, axis=1)
+        top = jnp.max(jnp.maximum(s_sel, s_own), axis=0, keepdims=True)
         e_sel = jnp.exp(s_sel - top)
         e_own = jnp.exp(s_own - top)
-        inv = 1.0 / jnp.sum(e_sel + e_own, axis=-1, keepdims=True)
+        inv = 1.0 / jnp.sum(e_sel + e_own, axis=0, keepdims=True)
         p_sel = e_sel * inv
         p_own = e_own * inv
-        prob[head, :, 0:PROMPT_LEN] = p_sel
-        prob[head, :, PROMPT_LEN:] = p_own
+        prob[head, 0:PROMPT_LEN] = p_sel
+        prob[head, PROMPT_LEN:] = p_own
         cs = stack(cv, head)
-        spread(gv, lanes, tn(p_sel.astype(BF), masked(cs)))
-        vlow[0:tokens, lanes] = tn(p_own.astype(BF), jnp.concatenate(cs, axis=0)).astype(BF)
-        return carry
+        spread(gv, lanes, nn(p_sel.astype(BF), masked(cs)))
+        vlow[0:tokens, lanes] = nn(p_own.astype(BF), jnp.concatenate(cs, axis=0)).astype(BF)
 
     def w_plane(dz):
         there = wfull.at[zat(dz), c, mine]
@@ -247,12 +248,18 @@
         there = wfull.at[zat(dz), c]
         go(rcopy(there, there, "w_c", dz, dz, partner))
 
-    lax.fori_loop(0, KV_HEADS // 2, softmax_head, 0)
-    for dz in range(1, nz):
+    softmax_head(0)
+    for dz in near:
         w_plane(dz)
-    lax.fori_loop(KV_HEADS // 2, KV_HEADS, softmax_head, 0)
+    softmax_head(1)
+    for dz in far:
+        w_plane(dz)
+    softmax_head(2)
+    for dz in near:
+        w_diagonal(dz)
+    softmax_head(3)
     scatter_pair(gv, gv_p, "rv_c")
-    for dz in range(1, nz):
+    for dz in far:
         w_diagonal(dz)
     gather_forward(dall, "d_z", "d_c")
     scatter_z(gv, gv_p, gv_h, gv_r, "rv_c", "rv_z")
@@ -272,10 +279,10 @@
         low[...] = lowest if first else low[...] + lowest
 
     forward(z, c, True)
-    for dz in range(1, nz):
+    for dz in near + far:
         w_chip(dz)
         forward(zat(dz), c, False)
-    for dz in range(nz):
+    for dz in [0] + near + far:
         there = wfull.at[zat(dz), oc]
         rcopy(there, there, "w_c", dz, dz, partner).wait_recv()
         forward(zat(dz), oc, False)
@@ -286,19 +293,6 @@
     vall[z, c] = values[tokens:]
     gather_start(vp, vall, "v_z", "v_c")
 
-    def back(first_row, count, out):
-        rows_here = vlow[first_row:first_row + count]
-        back_low = nt(rows_here, up[...]).astype(BF)
-
-        def one(at, carry):
-            z_at, c_at = at // 2, at % 2
-            out[:, columns(z_at, c_at)] = (
-                nt(rows_here, wfull[z_at, c_at]) + adapter_scale * nn(back_low, dall[z_at, c_at])).astype(BF)
-            return carry
-
-        lax.fori_loop(0, 2 * nz, one, 0)
-
-    back(0, tokens, o_rg)
     vlow[tokens:] = scatter_sum(gv_r, "rv_z").astype(BF)
     back_all = nt(vlow[...], up[...]).astype(BF)
     second = tn(first_proj, vlow[...]).astype(BF)
@@ -311,7 +305,15 @@
 
     lax.fori_loop(0, 2 * nz, adapter, 0)
     scatter_pair(ga, ga_p, "ra_c")
-    back(tokens, rows, o_pg)
+
+    def back(at, carry):
+        z_at, c_at = at // 2, at % 2
+        grad = (nt(vlow[...], wfull[z_at, c_at]) + adapter_scale * nn(back_all, dall[z_at, c_at])).astype(BF)
+        o_rg[:, columns(z_at, c_at)] = grad[:tokens]
+        o_pg[:, columns(z_at, c_at)] = grad[tokens:]
+        return carry
+
+    lax.fori_loop(0, 2 * nz, back, 0)
     gather_forward(vall, "v_z", "v_c")
     scatter_z(ga, ga_p, ga_h, ga_r, "ra_c", "ra_z")
     gather_finish(vall, "v_c")
@@ -319,26 +321,30 @@
     def key_head(head, carry):
         lanes = head_lanes(head)
         cs = stack(cv, head)
-        d_sel = nt(masked(cs), side(vall, lanes))
-        d_own = nt(jnp.concatenate(cs, axis=0), vloc[:, lanes])
-        p_sel = prob[head, :, 0:PROMPT_LEN]
-        p_own = prob[head, :, PROMPT_LEN:]
+        d_sel = nt(side(vall, lanes), masked(cs))
+        d_own = nt(vloc[:, lanes], jnp.concatenate(cs, axis=0))
+        p_sel = prob[head, 0:PROMPT_LEN]
+        p_own = prob[head, PROMPT_LEN:]
         delta = jnp.sum(p_sel.astype(BF).astype(F32) * d_sel + p_own.astype(BF).astype(F32) * d_own,
-                        axis=-1, keepdims=True)
+                        axis=0, keepdims=True)
         g_sel = (p_sel * (d_sel - delta)).astype(BF)
         g_own = (p_own * (d_own - delta)).astype(BF)
         qs = stack(qv, head)
-        spread(gk, lanes, tn(g_sel, masked(qs)) * SCORE_SCALE)
-        o_rk[:, lanes] = (tn(g_own, jnp.concatenate(qs, axis=0)) * SCORE_SCALE).astype(BF)
+        per_half = KV_HEADS // 2
+        spread(gk.at[head // per_half], head_lanes(head % per_half), nn(g_sel, masked(qs)) * SCORE_SCALE)
+        o_rk[:, lanes] = (nn(g_own, jnp.concatenate(qs, axis=0)) * SCORE_SCALE).astype(BF)
         return carry
 
-    lax.fori_loop(0, KV_HEADS, key_head, 0)
-    scatter_pair(gk, gk_p, "rk_c")
+    lax.fori_loop(0, KV_HEADS // 2, key_head, 0)
+    scatter_pair(gk.at[0], gk_p.at[0], "rk_c")
+    lax.fori_loop(KV_HEADS // 2, KV_HEADS, key_head, 0)
+    scatter_pair(gk.at[1], gk_p.at[1], "rk_c2")
+    scatter_z(gk.at[0], gk_p.at[0], gk_h.at[0], gk_r.at[0], "rk_c", "rk_z")
     gg[g] = scatter_sum(ga_r, "ra_z").astype(BF)
     for dg in range(1, n_group):
         there = lax.rem(g + dg, n_group)
         go(rcopy(gg.at[g], gg.at[g], "g", dg, n_group - dg, (there, j)))
-    scatter_z(gk, gk_p, gk_h, gk_r, "rk_c", "rk_z")
+    scatter_z(gk.at[1], gk_p.at[1], gk_h.at[1], gk_r.at[1], "rk_c2", "rk_z2")
     for dg in range(1, n_group):
         there = lax.rem(g + dg, n_group)
         rcopy(gg.at[there], gg.at[there], "g", dg, dg, (there, j)).wait_recv()
@@ -348,9 +354,20 @@
     total = total * factor
     o_f[...] = total[:, 0:shard]
     o_s[...] = total[:, shard:]
-    o_pk[...] = scatter_sum(gk_r, "rk_z").astype(BF)
+    width = o_pk.shape[1] // 2
+    o_pk[:, 0:width] = scatter_sum(gk_r.at[0], "rk_z").astype(BF)
+    o_pk[:, width:] = scatter_sum(gk_r.at[1], "rk_z2").astype(BF)
     for copy in sends:
         copy.wait_send()
+
+
+def store(*refs):
+    sem = refs[12]
+    copies = [pltpu.make_async_copy(refs[at], refs[6 + at], sem.at[at]) for at in range(6)]
+    for copy in copies:
+        copy.start()
+    for copy in copies:
+        copy.wait()
 
 
 def on_device(
@@ -369,24 +386,21 @@
     vmem = pl.BlockSpec(memory_space=pltpu.VMEM)
     smem = pl.BlockSpec(memory_space=pltpu.SMEM)
 
-    def reduce_space(high, across):
+    def reduce_space(high, across, lead=()):
         return [
-            pltpu.VMEM((nz, 2, high, across), BF),
-            pltpu.VMEM((nz, high, across), BF),
-            pltpu.VMEM((nz, high, across), BF),
-            pltpu.VMEM((nz, high, across), BF),
+            pltpu.VMEM((*lead, nz, 2, high, across), BF),
+            pltpu.VMEM((*lead, nz, high, across), BF),
+            pltpu.VMEM((*lead, nz, high, across), BF),
+            pltpu.VMEM((*lead, nz, high, across), BF),
         ]
 
+    shapes = (
+        ((tokens, d), BF), ((rows, d), BF), ((tokens, kv), BF), ((rows, kv), BF),
+        ((rank, shard), F32), ((rank, kv), F32),
+    )
     outs = pl.pallas_call(
         functools.partial(kernel, nz, n_group, places, factor),
-        out_shape=(
-            jax.ShapeDtypeStruct((tokens, d), BF),
-            jax.ShapeDtypeStruct((rows, d), BF),
-            jax.ShapeDtypeStruct((tokens, kv), BF),
-            jax.ShapeDtypeStruct((rows, kv), BF),
-            jax.ShapeDtypeStruct((rank, shard), F32),
-            jax.ShapeDtypeStruct((rank, kv), F32),
-        ),
+        out_shape=tuple(pltpu.VMEM(shape, kind) for shape, kind in shapes),
         in_specs=[any_space] * 5 + [vmem] * 3 + [smem] + [vmem] * 2,
         out_specs=(vmem,) * 6,
         scratch_shapes=[
@@ -399,14 +413,14 @@
             pltpu.VMEM((nz, 2, rank, shard), BF),
             pltpu.VMEM((n_sample * rows // PROMPT_LEN, tokens, HEAD_DIM), BF),
             pltpu.VMEM((tokens, tokens), F32),
-            pltpu.VMEM((KV_HEADS, GROUP_SIZE * tokens, PROMPT_LEN + tokens), F32),
+            pltpu.VMEM((KV_HEADS, PROMPT_LEN + tokens, GROUP_SIZE * tokens), F32),
             pltpu.VMEM((tokens + rows, kv), BF),
             pltpu.VMEM((tokens, kv), BF),
             pltpu.VMEM((rows, kv), BF),
             pltpu.VMEM((tokens + rows, kv), F32),
             pltpu.VMEM((tokens + rows, rank), F32),
             *reduce_space(rows, kv),
-            *reduce_space(rows, kv),
+            *reduce_space(rows, kv // 2, (2,)),
             *reduce_space(rank, wide),
             pltpu.VMEM((n_group, rank, wide), BF),
             pltpu.SemaphoreType.DMA((count,)),
@@ -420,6 +434,14 @@
         response_rows, prompt_rows, queries, cotangent, frozen_value_weight,
         response_keys, prompt_keys, segment_index, prompt_choice, value_adapter_down.T, value_adapter_up,
     )
+    outs = pl.pallas_call(
+        store,
+        out_shape=tuple(jax.ShapeDtypeStruct(shape, kind) for shape, kind in shapes),
+        in_specs=[any_space] * 6,
+        out_specs=(any_space,) * 6,
+        scratch_shapes=[pltpu.SemaphoreType.DMA((6,))],
+        name="store",
+    )(*outs)
     return (*outs[:4], outs[4].T, outs[5])
 
 

time: 71.3 us -> 123 us (1.73)
  Pallas kernels: 63.9 us -> 118 us
  local copies, waits for them, and re-layouts: 6.37 us -> 4.24 us
    pallas_call x0 -> x1, Pallas kernels: none -> 56.7 us  [on_device(): pl.pallas_call(store, out_shape=tuple((jax.ShapeDtypeStruct(shape, kind)...]
    pallas_call x1, Pallas kernels: 63.9 us -> 61.7 us  [on_device(): pl.pallas_call(functools.partial(kernel, nz, n_group, places, factor), ou...]
    unnamed x16 -> x12, local copies, waits for them, and re-layouts: 6.37 us -> 4.24 us
where the time goes in v2:
time: 123 us
  Pallas kernels  118 us (96%)
  local copies, waits for them, and re-layouts  4.24 us (3%)
    pallas_call x1, Pallas kernels, on_device(): pl.pallas_call(functools.partial(kernel, nz, n_group, places, factor), ou...  61.7 us
    pallas_call x1, Pallas kernels, on_device(): pl.pallas_call(store, out_shape=tuple((jax.ShapeDtypeStruct(shape, kind)...  56.7 us
    unnamed x12, local copies, waits for them, and re-layouts  4.24 us

profile of v2, /device:TPU:0, one launch (start us, length us, event | category | flops | bytes accessed | tf_op | source)
XLA Modules:
  0.0 123.3 jit_solution(17062931975375100568)
XLA Ops:
  0.6 61.7 %value_backward.1 = (bf16[128,4096]{1,0:T(8,128)(2,1)S(1)}, bf16[64,4096]{1,0:T(8,128)(2,1)S(1)}, bf16[128,512]{1,0:T(8,128)(2,1)S(1)}, bf16[64,512]{1,0:T(8,128...) custom-call(bf16[128,4096]{1,0:T(8,128)(2,1)} %xr.1, bf16[64,4096]{1,0:T(8,128)(2,1)} %xp.1, ...), custom_call_target="tpu_custom_call" | custom-call | tf_op jit(solution)/shard_map/value_backward/pallas_call | solution.py:401
  62.3 0.0 copy-start
  62.3 1.0 copy-done
  63.3 0.0 copy-start.1
  63.3 0.8 copy-done.1
  64.1 0.0 copy-start.2
  64.1 0.6 copy-done.2
  64.7 0.0 copy-start.3
  64.7 0.6 copy-done.3
  65.4 0.0 copy-start.4
  65.4 0.6 copy-done.4
  66.0 0.0 copy-start.5
  66.0 0.6 copy-done.5
  66.6 56.7 %store.1 = (bf16[128,4096]{1,0:T(8,128)(2,1)}, bf16[64,4096]{1,0:T(8,128)(2,1)}, bf16[128,512]{1,0:T(8,128)(2,1)}, bf16[64,512]{1,0:T(8,128)(2,1)}, f32[16,512]{1,0:T(8,128)}, /*index=5*/f32[16,512]{1,0:T(8,128)}) custom-call(bf16[128,4096]{1,0:T(8,128)(2,1)} %copy-done, bf16[64,4096]{1,0:T(8,128)(2,1)} %copy-done.1, bf16[128,512]{1,0:T(8,128)(2,1)} %copy-done.2, ...), custom_call_target="tpu_custom_call" | custom-call | tf_op jit(solution)/shard_map/store/pallas_call | solution.py:437
Async XLA Ops:
  62.3 1.0 copy-start
  63.3 0.8 copy-start.1
  64.1 0.6 copy-start.2
  64.7 0.6 copy-start.3
  65.4 0.6 copy-start.4
  66.0 0.6 copy-start.5

commit v3 on v2

--- a/solution.py
+++ b/solution.py
@@ -155,13 +155,13 @@
         pl.semaphore_signal(barrier, inc=1, device_id=(lax.rem(g + dg, n_group), j), device_id_type=MESH)
     pl.semaphore_wait(barrier, nz + n_group - 1)
 
-    gather_start(pk, kall, "k_z", "k_c")
     mine = pl.ds(pl.multiple_of(qme * quarter, 16), quarter)
     for dz in near + far:
         go(rcopy(w.at[mine], wfull.at[z, c, mine], "w_z", dz, nz - dz, zdev(dz)))
     go(rcopy(w, wfull.at[z, c], "w_c", 0, 0, partner))
     own_w = pltpu.make_async_copy(w, wfull.at[z, c], ssem.at[places["w_z"]])
     own_w.start()
+    gather_start(pk, kall, "k_z", "k_c")
 
     dall[z, c] = dn[...]
     gather_start(dn, dall, "d_z", "d_c")
@@ -177,11 +177,6 @@
         choice = jnp.where(seg_col == float(at), ch[0, at], choice)
     for at in range(prompts):
         pmask[at] = jnp.where(choice == at, 1.0, 0.0).astype(BF)
-
-    gather_forward(kall, "k_z", "k_c")
-    local[0].wait()
-    local[1].wait()
-    gather_finish(kall, "k_c")
 
     def stack(ref, head):
         return [ref[:, pl.ds(pl.multiple_of((head * GROUP_SIZE + at) * HEAD_DIM, HEAD_DIM), HEAD_DIM)]
@@ -248,26 +243,6 @@
         there = wfull.at[zat(dz), c]
         go(rcopy(there, there, "w_c", dz, dz, partner))
 
-    softmax_head(0)
-    for dz in near:
-        w_plane(dz)
-    softmax_head(1)
-    for dz in far:
-        w_plane(dz)
-    softmax_head(2)
-    for dz in near:
-        w_diagonal(dz)
-    softmax_head(3)
-    scatter_pair(gv, gv_p, "rv_c")
-    for dz in far:
-        w_diagonal(dz)
-    gather_forward(dall, "d_z", "d_c")
-    scatter_z(gv, gv_p, gv_h, gv_r, "rv_c", "rv_z")
-    local[2].wait()
-    local[3].wait()
-    own_w.wait()
-    gather_finish(dall, "d_c")
-
     def columns(z_at, c_at):
         return pl.ds(pl.multiple_of((2 * z_at + c_at) * shard, 128), shard)
 
@@ -278,14 +253,30 @@
         acc[...] = base if first else acc[...] + base
         low[...] = lowest if first else low[...] + lowest
 
+    def forward_other(dz):
+        there = wfull.at[zat(dz), oc]
+        rcopy(there, there, "w_c", dz, dz, partner).wait_recv()
+        forward(zat(dz), oc, False)
+
+    for dz in near:
+        w_plane(dz)
+    gather_forward(dall, "d_z", "d_c")
+    gather_finish(dall, "d_c")
+    local[2].wait()
+    local[3].wait()
+    own_w.wait()
     forward(z, c, True)
+    forward_other(0)
+    for dz in far:
+        w_plane(dz)
+    for dz in near + far:
+        w_diagonal(dz)
+    gather_forward(kall, "k_z", "k_c")
     for dz in near + far:
         w_chip(dz)
         forward(zat(dz), c, False)
-    for dz in [0] + near + far:
-        there = wfull.at[zat(dz), oc]
-        rcopy(there, there, "w_c", dz, dz, partner).wait_recv()
-        forward(zat(dz), oc, False)
+    for dz in near + far:
+        forward_other(dz)
     first_proj = low[...].astype(BF)
     values = (acc[...] + adapter_scale * nn(first_proj, up[...])).astype(BF)
     vp[...] = values[tokens:]
@@ -293,30 +284,16 @@
     vall[z, c] = values[tokens:]
     gather_start(vp, vall, "v_z", "v_c")
 
-    vlow[tokens:] = scatter_sum(gv_r, "rv_z").astype(BF)
-    back_all = nt(vlow[...], up[...]).astype(BF)
-    second = tn(first_proj, vlow[...]).astype(BF)
-
-    def adapter(at, carry):
-        z_at, c_at = at // 2, at % 2
-        ga[z_at, c_at, :, 0:shard] = tn(back_all, xv[:, columns(z_at, c_at)]).astype(BF)
-        ga[z_at, c_at, :, shard:] = second
-        return carry
-
-    lax.fori_loop(0, 2 * nz, adapter, 0)
-    scatter_pair(ga, ga_p, "ra_c")
-
-    def back(at, carry):
-        z_at, c_at = at // 2, at % 2
-        grad = (nt(vlow[...], wfull[z_at, c_at]) + adapter_scale * nn(back_all, dall[z_at, c_at])).astype(BF)
-        o_rg[:, columns(z_at, c_at)] = grad[:tokens]
-        o_pg[:, columns(z_at, c_at)] = grad[tokens:]
-        return carry
-
-    lax.fori_loop(0, 2 * nz, back, 0)
-    gather_forward(vall, "v_z", "v_c")
-    scatter_z(ga, ga_p, ga_h, ga_r, "ra_c", "ra_z")
+    local[0].wait()
+    local[1].wait()
+    gather_finish(kall, "k_c")
+    for head in range(KV_HEADS):
+        softmax_head(head)
+        if head == KV_HEADS // 2:
+            gather_forward(vall, "v_z", "v_c")
+    scatter_pair(gv, gv_p, "rv_c")
     gather_finish(vall, "v_c")
+    scatter_z(gv, gv_p, gv_h, gv_r, "rv_c", "rv_z")
 
     def key_head(head, carry):
         lanes = head_lanes(head)
@@ -337,14 +314,38 @@
 
     lax.fori_loop(0, KV_HEADS // 2, key_head, 0)
     scatter_pair(gk.at[0], gk_p.at[0], "rk_c")
+
+    vlow[tokens:] = scatter_sum(gv_r, "rv_z").astype(BF)
+    back_all = nt(vlow[...], up[...]).astype(BF)
+    second = tn(first_proj, vlow[...]).astype(BF)
+
+    def adapter(at, carry):
+        z_at, c_at = at // 2, at % 2
+        ga[z_at, c_at, :, 0:shard] = tn(back_all, xv[:, columns(z_at, c_at)]).astype(BF)
+        ga[z_at, c_at, :, shard:] = second
+        return carry
+
+    lax.fori_loop(0, 2 * nz, adapter, 0)
+    scatter_pair(ga, ga_p, "ra_c")
+    scatter_z(gk.at[0], gk_p.at[0], gk_h.at[0], gk_r.at[0], "rk_c", "rk_z")
     lax.fori_loop(KV_HEADS // 2, KV_HEADS, key_head, 0)
     scatter_pair(gk.at[1], gk_p.at[1], "rk_c2")
-    scatter_z(gk.at[0], gk_p.at[0], gk_h.at[0], gk_r.at[0], "rk_c", "rk_z")
+    scatter_z(ga, ga_p, ga_h, ga_r, "ra_c", "ra_z")
+    scatter_z(gk.at[1], gk_p.at[1], gk_h.at[1], gk_r.at[1], "rk_c2", "rk_z2")
+
+    def back(at, carry):
+        z_at, c_at = at // 2, at % 2
+        grad = (nt(vlow[...], wfull[z_at, c_at]) + adapter_scale * nn(back_all, dall[z_at, c_at])).astype(BF)
+        o_rg[:, columns(z_at, c_at)] = grad[:tokens]
+        o_pg[:, columns(z_at, c_at)] = grad[tokens:]
+        return carry
+
+    lax.fori_loop(0, nz, back, 0)
     gg[g] = scatter_sum(ga_r, "ra_z").astype(BF)
     for dg in range(1, n_group):
         there = lax.rem(g + dg, n_group)
         go(rcopy(gg.at[g], gg.at[g], "g", dg, n_group - dg, (there, j)))
-    scatter_z(gk.at[1], gk_p.at[1], gk_h.at[1], gk_r.at[1], "rk_c2", "rk_z2")
+    lax.fori_loop(nz, 2 * nz, back, 0)
     for dg in range(1, n_group):
         there = lax.rem(g + dg, n_group)
         rcopy(gg.at[there], gg.at[there], "g", dg, dg, (there, j)).wait_recv()
@@ -437,8 +438,8 @@
     outs = pl.pallas_call(
         store,
         out_shape=tuple(jax.ShapeDtypeStruct(shape, kind) for shape, kind in shapes),
-        in_specs=[any_space] * 6,
-        out_specs=(any_space,) * 6,
+        in_specs=[vmem] * 6,
+        out_specs=(pl.BlockSpec(memory_space=pltpu.HBM),) * 6,
         scratch_shapes=[pltpu.SemaphoreType.DMA((6,))],
         name="store",
     )(*outs)

time: 123 us -> 77.3 us (0.63)
  Pallas kernels: 118 us -> 72.2 us
    pallas_call x1, Pallas kernels: 56.7 us -> 2.67 us  [on_device(): pl.pallas_call(store, out_shape=tuple((jax.ShapeDtypeStruct(shape, kind)...]
    pallas_call x1, Pallas kernels: 61.7 us -> 69.5 us  [on_device(): pl.pallas_call(functools.partial(kernel, nz, n_group, places, factor), ou...]
where the time goes in v3:
time: 77.3 us; the launch traced here: 77.1 us
  Pallas kernels  72.2 us (93%)
  local copies, waits for them, and re-layouts  4.24 us (5%)
    pallas_call x1, Pallas kernels, on_device(): pl.pallas_call(functools.partial(kernel, nz, n_group, places, factor), ou...  69.5 us
    unnamed x12, local copies, waits for them, and re-layouts  4.24 us
    pallas_call x1, Pallas kernels, on_device(): pl.pallas_call(store, out_shape=tuple((jax.ShapeDtypeStruct(shape, kind)...  2.67 us

profile of v3, /device:TPU:0, one launch (start us, length us, event | category | flops | bytes accessed | tf_op | source)
XLA Modules:
  0.0 77.1 jit_solution(10106182623196983659)
XLA Ops:
  0.6 69.5 %value_backward.1 = (bf16[128,4096]{1,0:T(8,128)(2,1)S(1)}, bf16[64,4096]{1,0:T(8,128)(2,1)S(1)}, bf16[128,512]{1,0:T(8,128)(2,1)S(1)}, bf16[64,512]{1,0:T(8,128...) custom-call(bf16[128,4096]{1,0:T(8,128)(2,1)} %xr.1, bf16[64,4096]{1,0:T(8,128)(2,1)} %xp.1, ...), custom_call_target="tpu_custom_call" | custom-call | tf_op jit(solution)/shard_map/value_backward/pallas_call | solution.py:402
  70.2 0.0 copy-start
  70.2 1.0 %copy-done = bf16[128,4096]{1,0:T(8,128)(2,1)} copy-done((bf16[128,4096]{1,0:T(8,128)(2,1)}, bf16[128,4096]{1,0:T(8,128)(2,1)S(1)}, u32[]{:S(2)}) %copy-start) | copy-done | bytes 1048600
  71.1 0.0 copy-start.1
  71.1 0.8 %copy-done.1 = bf16[64,4096]{1,0:T(8,128)(2,1)} copy-done((bf16[64,4096]{1,0:T(8,128)(2,1)}, bf16[64,4096]{1,0:T(8,128)(2,1)S(1)}, u32[]{:S(2)}) %copy-start.1) | copy-done | bytes 524312
  71.9 0.0 copy-start.2
  71.9 0.6 copy-done.2
  72.6 0.0 copy-start.3
  72.6 0.6 copy-done.3
  73.2 0.0 copy-start.4
  73.2 0.6 copy-done.4
  73.8 0.0 copy-start.5
  73.8 0.6 copy-done.5
  74.4 2.7 %store.1 = (bf16[128,4096]{1,0:T(8,128)(2,1)}, bf16[64,4096]{1,0:T(8,128)(2,1)}, bf16[128,512]{1,0:T(8,128)(2,1)}, bf16[64,512]{1,0:T(8,128)(2,1)}, f32[16,512]{1,0:T(8,128)}, /*index=5*/f32[16,512]{1,0:T(8,128)}) custom-call(bf16[128,4096]{1,0:T(8,128)(2,1)} %copy-done, bf16[64,4096]{1,0:T(8,128)(2,1)} %copy-done.1, bf16[128,512]{1,0:T(8,128)(2,1)} %copy-done.2, ...), custom_call_target="tpu_custom_call" | custom-call | tf_op jit(solution)/shard_map/store/pallas_call | solution.py:438
Async XLA Ops:
  70.2 1.0 %copy-start = (bf16[128,4096]{1,0:T(8,128)(2,1)}, bf16[128,4096]{1,0:T(8,128)(2,1)S(1)}, u32[]{:S(2)}) copy-start(bf16[128,4096]{1,0:T(8,128)(2,1)S(1)} %get-tuple-element.18.refs_0_) | copy-start | bytes 3145732
  71.1 0.8 %copy-start.1 = (bf16[64,4096]{1,0:T(8,128)(2,1)}, bf16[64,4096]{1,0:T(8,128)(2,1)S(1)}, u32[]{:S(2)}) copy-start(bf16[64,4096]{1,0:T(8,128)(2,1)S(1)} %get-tuple-element.19.refs_1_) | copy-start | bytes 1572868
  71.9 0.6 copy-start.2
  72.6 0.6 copy-start.3
  73.2 0.6 copy-start.4
  73.8 0.6 copy-start.5

commit v4 on v2

--- a/solution.py
+++ b/solution.py
@@ -46,14 +46,14 @@
 def layout(nz, n_group):
     slots = Slots()
     places = {name: slots.take(nz) for name in (
-        "k_z", "k_c", "d_z", "d_c", "v_z", "v_c",
+        "k_z", "k_l", "k_c", "w_l", "d_z", "d_c", "v_z", "v_c",
         "w_z", "w_c", "w_x", "w_y", "w_d0", "w_d1",
         "rv_z", "rk_z", "rk_z2", "ra_z",
     )}
     for name in ("rv_c", "rk_c", "rk_c2", "ra_c"):
         places[name] = slots.take(1)
     places["g"] = slots.take(n_group)
-    places["local"] = slots.take(4)
+    places["local"] = slots.take(5)
     return places, slots.count
 
 
@@ -89,20 +89,46 @@
     def zdev(dz):
         return (g, 2 * zat(dz) + c)
 
-    def rcopy(src, dst, name, send, recv, device):
+    def rcopy(src, dst, name, send, recv, device, recv_name=None):
         return pltpu.make_async_remote_copy(
             src_ref=src, dst_ref=dst,
-            send_sem=ssem.at[places[name] + send], recv_sem=rsem.at[places[name] + recv],
+            send_sem=ssem.at[places[name] + send], recv_sem=rsem.at[places[recv_name or name] + recv],
             device_id=device, device_id_type=MESH,
         )
 
-    near = [dz for dz in range(1, nz) if dz in (1, nz - 1)]
-    far = [dz for dz in range(1, nz) if dz not in near]
+    short = jnp.minimum(z, nz - 1 - z)
+
+    def source(k):
+        alternate = z + (k + 1) // 2 if k % 2 else z - k // 2
+        one_side = jnp.where(2 * z < nz - 1, z + k - short, z - k + short)
+        return jnp.where(k <= 2 * short, alternate, one_side)
+
+    sources = [source(k) for k in range(1, nz)]
+
     sends = []
 
     def go(copy):
         copy.start()
         sends.append(copy)
+
+    waits = []
+
+    def go_if(condition, make):
+        @pl.when(condition)
+        def _():
+            make().start()
+
+        waits.append((condition, make))
+
+    def chain_start(src, dst, name, name_left):
+        go_if(z + 1 < nz, lambda: rcopy(src, dst, name, z, z, (g, jnp.minimum(j + 2, 2 * nz - 1))))
+        go_if(z >= 1, lambda: rcopy(src, dst, name_left, z, z, (g, jnp.maximum(j - 2, 0)), name))
+
+    def chain_next(there, name, src):
+        rcopy(there, there, name, src, src, partner).wait_recv()
+        after = jnp.where(src < z, z + 1, z - 1)
+        inside = jnp.minimum(jnp.maximum(after, 0), nz - 1)
+        go_if(after == inside, lambda: rcopy(there, there, name, src, src, (g, 2 * inside + c)))
 
     def gather_start(src, buf, name_z, name_c):
         for dz in range(1, nz):
@@ -155,12 +181,12 @@
         pl.semaphore_signal(barrier, inc=1, device_id=(lax.rem(g + dg, n_group), j), device_id_type=MESH)
     pl.semaphore_wait(barrier, nz + n_group - 1)
 
-    gather_start(pk, kall, "k_z", "k_c")
     mine = pl.ds(pl.multiple_of(qme * quarter, 16), quarter)
-    for dz in near + far:
-        go(rcopy(w.at[mine], wfull.at[z, c, mine], "w_z", dz, nz - dz, zdev(dz)))
-    go(rcopy(w, wfull.at[z, c], "w_c", 0, 0, partner))
-    own_w = pltpu.make_async_copy(w, wfull.at[z, c], ssem.at[places["w_z"]])
+    chain_start(pk, kall.at[z, c], "k_z", "k_l")
+    go(rcopy(pk, kall.at[z, c], "k_c", z, z, partner))
+    chain_start(w.at[mine], wfull.at[z, c, mine], "w_z", "w_l")
+    go(rcopy(w, wfull.at[z, c], "w_c", z, z, partner))
+    own_w = pltpu.make_async_copy(w, wfull.at[z, c], ssem.at[places["local"] + 4])
     own_w.start()
 
     dall[z, c] = dn[...]
@@ -177,11 +203,6 @@
         choice = jnp.where(seg_col == float(at), ch[0, at], choice)
     for at in range(prompts):
         pmask[at] = jnp.where(choice == at, 1.0, 0.0).astype(BF)
-
-    gather_forward(kall, "k_z", "k_c")
-    local[0].wait()
-    local[1].wait()
-    gather_finish(kall, "k_c")
 
     def stack(ref, head):
         return [ref[:, pl.ds(pl.multiple_of((head * GROUP_SIZE + at) * HEAD_DIM, HEAD_DIM), HEAD_DIM)]
@@ -222,51 +243,62 @@
         spread(gv, lanes, nn(p_sel.astype(BF), masked(cs)))
         vlow[0:tokens, lanes] = nn(p_own.astype(BF), jnp.concatenate(cs, axis=0)).astype(BF)
 
-    def w_plane(dz):
-        there = wfull.at[zat(dz), c, mine]
-        rcopy(there, there, "w_z", dz, dz, zdev(dz)).wait_recv()
-        go(rcopy(there, there, "w_x", dz, dz, (gx, j)))
-        go(rcopy(there, there, "w_y", dz, dz, (gy, j)))
-
-    def w_diagonal(dz):
-        at_x = pl.ds(pl.multiple_of(qx * quarter, 16), quarter)
-        at_y = pl.ds(pl.multiple_of(qy * quarter, 16), quarter)
-        there = wfull.at[zat(dz), c, at_x]
-        rcopy(there, there, "w_x", dz, dz, (gx, j)).wait_recv()
-        first = wfull.at[zat(dz), c, pl.ds(pl.multiple_of(qx * quarter, 16), half)]
-        go(rcopy(first, first, "w_d0", dz, dz, (gy, j)))
-        there = wfull.at[zat(dz), c, at_y]
-        rcopy(there, there, "w_y", dz, dz, (gy, j)).wait_recv()
-        second = wfull.at[zat(dz), c, pl.ds(pl.multiple_of(qy * quarter + half, 16), half)]
-        go(rcopy(second, second, "w_d1", dz, dz, (gx, j)))
-
-    def w_chip(dz):
-        first = wfull.at[zat(dz), c, pl.ds(pl.multiple_of(qd * quarter, 16), half)]
-        rcopy(first, first, "w_d0", dz, dz, (gy, j)).wait_recv()
-        second = wfull.at[zat(dz), c, pl.ds(pl.multiple_of(qd * quarter + half, 16), half)]
-        rcopy(second, second, "w_d1", dz, dz, (gx, j)).wait_recv()
-        there = wfull.at[zat(dz), c]
-        go(rcopy(there, there, "w_c", dz, dz, partner))
-
-    softmax_head(0)
-    for dz in near:
-        w_plane(dz)
-    softmax_head(1)
-    for dz in far:
-        w_plane(dz)
-    softmax_head(2)
-    for dz in near:
-        w_diagonal(dz)
-    softmax_head(3)
+    def w_plane(src):
+        there = wfull.at[src, c, mine]
+        chain_next(there, "w_z", src)
+        go(rcopy(there, there, "w_x", src, src, (gx, j)))
+        go(rcopy(there, there, "w_y", src, src, (gy, j)))
+
+    def w_diagonal(src):
+        there = wfull.at[src, c, pl.ds(pl.multiple_of(qx * quarter, 16), quarter)]
+        rcopy(there, there, "w_x", src, src, (gx, j)).wait_recv()
+        first = wfull.at[src, c, pl.ds(pl.multiple_of(qx * quarter, 16), half)]
+        go(rcopy(first, first, "w_d0", src, src, (gy, j)))
+        there = wfull.at[src, c, pl.ds(pl.multiple_of(qy * quarter, 16), quarter)]
+        rcopy(there, there, "w_y", src, src, (gy, j)).wait_recv()
+        second = wfull.at[src, c, pl.ds(pl.multiple_of(qy * quarter + half, 16), half)]
+        go(rcopy(second, second, "w_d1", src, src, (gx, j)))
+
+    def w_chip(src):
+        first = wfull.at[src, c, pl.ds(pl.multiple_of(qd * quarter, 16), half)]
+        rcopy(first, first, "w_d0", src, src, (gy, j)).wait_recv()
+        second = wfull.at[src, c, pl.ds(pl.multiple_of(qd * quarter + half, 16), half)]
+        rcopy(second, second, "w_d1", src, src, (gx, j)).wait_recv()
+        there = wfull.at[src, c]
+        go(rcopy(there, there, "w_c", src, src, partner))
+
+    for src in sources:
+        there = kall.at[src, c]
+        chain_next(there, "k_z", src)
+        go(rcopy(there, there, "k_c", src, src, partner))
+    local[0].wait()
+    local[1].wait()
+    for at in range(nz):
+        there = kall.at[at, oc]
+        rcopy(there, there, "k_c", at, at, partner).wait_recv()
+
+    stages = []
+    for at in range(nz + 1):
+        if at < nz - 1:
+            stages.append(functools.partial(w_plane, sources[at]))
+        if 0 <= at - 1 < nz - 1:
+            stages.append(functools.partial(w_diagonal, sources[at - 1]))
+        if 0 <= at - 2 < nz - 1:
+            stages.append(functools.partial(w_chip, sources[at - 2]))
+    per_head = -(-len(stages) // (KV_HEADS + 1))
+    for head in range(KV_HEADS):
+        for stage in stages[head * per_head:(head + 1) * per_head]:
+            stage()
+        softmax_head(head)
     scatter_pair(gv, gv_p, "rv_c")
-    for dz in far:
-        w_diagonal(dz)
+    for stage in stages[KV_HEADS * per_head:]:
+        stage()
     gather_forward(dall, "d_z", "d_c")
     scatter_z(gv, gv_p, gv_h, gv_r, "rv_c", "rv_z")
+    gather_finish(dall, "d_c")
     local[2].wait()
     local[3].wait()
     own_w.wait()
-    gather_finish(dall, "d_c")
 
     def columns(z_at, c_at):
         return pl.ds(pl.multiple_of((2 * z_at + c_at) * shard, 128), shard)
@@ -279,13 +311,12 @@
         low[...] = lowest if first else low[...] + lowest
 
     forward(z, c, True)
-    for dz in near + far:
-        w_chip(dz)
-        forward(zat(dz), c, False)
-    for dz in [0] + near + far:
-        there = wfull.at[zat(dz), oc]
-        rcopy(there, there, "w_c", dz, dz, partner).wait_recv()
-        forward(zat(dz), oc, False)
+    for src in sources:
+        forward(src, c, False)
+    for src in [z] + sources:
+        there = wfull.at[src, oc]
+        rcopy(there, there, "w_c", src, src, partner).wait_recv()
+        forward(src, oc, False)
     first_proj = low[...].astype(BF)
     values = (acc[...] + adapter_scale * nn(first_proj, up[...])).astype(BF)
     vp[...] = values[tokens:]
@@ -313,7 +344,7 @@
         o_pg[:, columns(z_at, c_at)] = grad[tokens:]
         return carry
 
-    lax.fori_loop(0, 2 * nz, back, 0)
+    lax.fori_loop(0, nz, back, 0)
     gather_forward(vall, "v_z", "v_c")
     scatter_z(ga, ga_p, ga_h, ga_r, "ra_c", "ra_z")
     gather_finish(vall, "v_c")
@@ -337,14 +368,16 @@
 
     lax.fori_loop(0, KV_HEADS // 2, key_head, 0)
     scatter_pair(gk.at[0], gk_p.at[0], "rk_c")
-    lax.fori_loop(KV_HEADS // 2, KV_HEADS, key_head, 0)
-    scatter_pair(gk.at[1], gk_p.at[1], "rk_c2")
+    lax.fori_loop(KV_HEADS // 2, KV_HEADS - 1, key_head, 0)
     scatter_z(gk.at[0], gk_p.at[0], gk_h.at[0], gk_r.at[0], "rk_c", "rk_z")
     gg[g] = scatter_sum(ga_r, "ra_z").astype(BF)
     for dg in range(1, n_group):
         there = lax.rem(g + dg, n_group)
         go(rcopy(gg.at[g], gg.at[g], "g", dg, n_group - dg, (there, j)))
+    lax.fori_loop(KV_HEADS - 1, KV_HEADS, key_head, 0)
+    scatter_pair(gk.at[1], gk_p.at[1], "rk_c2")
     scatter_z(gk.at[1], gk_p.at[1], gk_h.at[1], gk_r.at[1], "rk_c2", "rk_z2")
+    lax.fori_loop(nz, 2 * nz, back, 0)
     for dg in range(1, n_group):
         there = lax.rem(g + dg, n_group)
         rcopy(gg.at[there], gg.at[there], "g", dg, dg, (there, j)).wait_recv()
@@ -359,6 +392,10 @@
     o_pk[:, width:] = scatter_sum(gk_r.at[1], "rk_z2").astype(BF)
     for copy in sends:
         copy.wait_send()
+    for condition, make in waits:
+        @pl.when(condition)
+        def _():
+            make().wait_send()
 
 
 def store(*refs):
@@ -400,7 +437,7 @@
     )
     outs = pl.pallas_call(
         functools.partial(kernel, nz, n_group, places, factor),
-        out_shape=tuple(pltpu.VMEM(shape, kind) for shape, kind in shapes),
+        out_shape=tuple(jax.ShapeDtypeStruct(shape, kind) for shape, kind in shapes),
         in_specs=[any_space] * 5 + [vmem] * 3 + [smem] + [vmem] * 2,
         out_specs=(vmem,) * 6,
         scratch_shapes=[
@@ -437,8 +474,8 @@
     outs = pl.pallas_call(
         store,
         out_shape=tuple(jax.ShapeDtypeStruct(shape, kind) for shape, kind in shapes),
-        in_specs=[any_space] * 6,
-        out_specs=(any_space,) * 6,
+        in_specs=[vmem] * 6,
+        out_specs=(pl.BlockSpec(memory_space=pltpu.HBM),) * 6,
         scratch_shapes=[pltpu.SemaphoreType.DMA((6,))],
         name="store",
     )(*outs)

time: 123 us -> 63.9 us (0.52)
  Pallas kernels: 118 us -> 63.1 us
  local copies, waits for them, and re-layouts: 4.24 us -> 0 us
    pallas_call x1, Pallas kernels: 56.7 us -> 2.68 us  [on_device(): pl.pallas_call(store, out_shape=tuple((jax.ShapeDtypeStruct(shape, kind)...]
    unnamed x12 -> x0, local copies, waits for them, and re-layouts: 4.24 us -> none
    pallas_call x1, Pallas kernels: 61.7 us -> 60.4 us  [on_device(): pl.pallas_call(functools.partial(kernel, nz, n_group, places, factor), ou...]
where the time goes in v4:
time: 63.9 us; the launch traced here: 63.7 us
  Pallas kernels  63.1 us (99%)
  between operations  0.64 us (1%)
    pallas_call x1, Pallas kernels, on_device(): pl.pallas_call(functools.partial(kernel, nz, n_group, places, factor), ou...  60.4 us
    pallas_call x1, Pallas kernels, on_device(): pl.pallas_call(store, out_shape=tuple((jax.ShapeDtypeStruct(shape, kind)...  2.68 us

profile of v4, /device:TPU:0, one launch (start us, length us, event | category | flops | bytes accessed | tf_op | source)
XLA Modules:
  0.0 63.7 jit_solution(9970587191669209231)
XLA Ops:
  0.6 60.4 %value_backward.1 = (bf16[128,4096]{1,0:T(8,128)(2,1)}, bf16[64,4096]{1,0:T(8,128)(2,1)}, bf16[128,512]{1,0:T(8,128)(2,1)}, bf16[64,512]{1,0:T(8,128)(2,1)}, f32[16,512]{1,0:T(8,128)}, /*index=5*/f32[16,512]{1,0:T(8,128)}) custom-call(bf16[128,4096]{1,0:T(8,128)(2,1)} %xr.1, bf16[64,4096]{1,0:T(8,128)(2,1)} %xp.1, bf16[128,4096]{1,0:T(8,128)(2,1)} %q.1, ...), custom_call_target="tpu_custom_call" | custom-call | tf_op jit(solution)/shard_map/value_backward/pallas_call | solution.py:438
  61.1 2.7 %store.1 = (bf16[128,4096]{1,0:T(8,128)(2,1)}, bf16[64,4096]{1,0:T(8,128)(2,1)}, bf16[128,512]{1,0:T(8,128)(2,1)}, bf16[64,512]{1,0:T(8,128)(2,1)}, f32[16,512]{1,0:T(8,128)}, /*index=5*/f32[16,512]{1,0:T(8,128)}) custom-call(bf16[128,4096]{1,0:T(8,128)(2,1)} %get-tuple-element.18.refs_0_, bf16[64,4096]{1,0:T(8,128)(2,1)} %get-tuple-element.19.refs_1_, ...), custom_call_target="tpu_custom_call" | custom-call | tf_op jit(solution)/shard_map/store/pallas_call | solution.py:474

commit v5 on v4

--- a/solution.py
+++ b/solution.py
@@ -61,7 +61,7 @@
     nz, n_group, places, factor,
     xr, xp, q, ct, w, rk, pk, seg, ch, dn, up,
     o_rg, o_pg, o_rk, o_pk, o_f, o_s,
-    xv, qv, cv, wfull, kall, vall, dall, pmask, obias, prob, vlow, vloc, vp, acc, low,
+    xv, qv, cv, wfull, kall, vall, dall, pmask, obias, prob, vlow, vloc, vp, acc,
     gv, gv_p, gv_h, gv_r, gk, gk_p, gk_h, gk_r, ga, ga_p, ga_h, ga_r, gg,
     ssem, rsem,
 ):
@@ -217,6 +217,15 @@
             [buf[at * nzp:(at + 1) * nzp, :, :, lanes].reshape(PROMPT_LEN, HEAD_DIM) for at in range(prompts)],
             axis=1)
 
+    def with_own(prompt_side, own):
+        return jnp.concatenate([prompt_side, jnp.concatenate([own] * prompts, axis=1)], axis=0)
+
+    def own_sum(grads):
+        total = grads[PROMPT_LEN:, 0:HEAD_DIM]
+        for at in range(1, prompts):
+            total = total + grads[PROMPT_LEN:, at * HEAD_DIM:(at + 1) * HEAD_DIM]
+        return total
+
     def head_lanes(head):
         return pl.ds(pl.multiple_of(head * HEAD_DIM, HEAD_DIM), HEAD_DIM)
 
@@ -228,9 +237,9 @@
     def softmax_head(head):
         lanes = head_lanes(head)
         qs = stack(qv, head)
-        s_sel = nt(side(kall, lanes), masked(qs)) * SCORE_SCALE
-        s_own = nt(rk[:, lanes], jnp.concatenate(qs, axis=0)) * SCORE_SCALE
-        s_own = s_own + jnp.concatenate([obias[...]] * GROUP_SIZE, axis=1)
+        scores = nt(with_own(side(kall, lanes), rk[:, lanes]), masked(qs)) * SCORE_SCALE
+        s_sel = scores[:PROMPT_LEN]
+        s_own = scores[PROMPT_LEN:] + jnp.concatenate([obias[...]] * GROUP_SIZE, axis=1)
         top = jnp.max(jnp.maximum(s_sel, s_own), axis=0, keepdims=True)
         e_sel = jnp.exp(s_sel - top)
         e_own = jnp.exp(s_own - top)
@@ -240,8 +249,9 @@
         prob[head, 0:PROMPT_LEN] = p_sel
         prob[head, PROMPT_LEN:] = p_own
         cs = stack(cv, head)
-        spread(gv, lanes, nn(p_sel.astype(BF), masked(cs)))
-        vlow[0:tokens, lanes] = nn(p_own.astype(BF), jnp.concatenate(cs, axis=0)).astype(BF)
+        grads = nn(jnp.concatenate([p_sel.astype(BF), p_own.astype(BF)], axis=0), masked(cs))
+        spread(gv, lanes, grads[:PROMPT_LEN])
+        vlow[0:tokens, lanes] = own_sum(grads).astype(BF)
 
     def w_plane(src):
         there = wfull.at[src, c, mine]
@@ -277,22 +287,19 @@
         there = kall.at[at, oc]
         rcopy(there, there, "k_c", at, at, partner).wait_recv()
 
-    stages = []
-    for at in range(nz + 1):
-        if at < nz - 1:
-            stages.append(functools.partial(w_plane, sources[at]))
-        if 0 <= at - 1 < nz - 1:
-            stages.append(functools.partial(w_diagonal, sources[at - 1]))
-        if 0 <= at - 2 < nz - 1:
-            stages.append(functools.partial(w_chip, sources[at - 2]))
-    per_head = -(-len(stages) // (KV_HEADS + 1))
+    last = nz - 2
     for head in range(KV_HEADS):
-        for stage in stages[head * per_head:(head + 1) * per_head]:
-            stage()
+        for at in range(nz - 1):
+            if min(at, KV_HEADS - 1) == head:
+                w_plane(sources[at])
+        for at in range(last):
+            if min(at + 1, KV_HEADS - 1) == head:
+                w_diagonal(sources[at])
         softmax_head(head)
     scatter_pair(gv, gv_p, "rv_c")
-    for stage in stages[KV_HEADS * per_head:]:
-        stage()
+    w_diagonal(sources[last])
+    for at in range(last):
+        w_chip(sources[at])
     gather_forward(dall, "d_z", "d_c")
     scatter_z(gv, gv_p, gv_h, gv_r, "rv_c", "rv_z")
     gather_finish(dall, "d_c")
@@ -303,39 +310,48 @@
     def columns(z_at, c_at):
         return pl.ds(pl.multiple_of((2 * z_at + c_at) * shard, 128), shard)
 
+    def low_part(z_at, c_at):
+        return nt(xv[:, columns(z_at, c_at)], dall[z_at, c_at])
+
+    def low_step(at, carry):
+        return carry + low_part(at // 2, at % 2)
+
+    first_proj = lax.fori_loop(1, 2 * nz, low_step, low_part(0, 0)).astype(BF)
+
     def forward(z_at, c_at, first):
-        x = xv[:, columns(z_at, c_at)]
-        base = nn(x, wfull[z_at, c_at])
-        lowest = nt(x, dall[z_at, c_at])
+        base = nn(xv[:, columns(z_at, c_at)], wfull[z_at, c_at])
         acc[...] = base if first else acc[...] + base
-        low[...] = lowest if first else low[...] + lowest
 
     forward(z, c, True)
+    w_chip(sources[last])
+    rcopy(wfull.at[z, oc], wfull.at[z, oc], "w_c", z, z, partner).wait_recv()
+    forward(z, oc, False)
+    for src in sources[:last]:
+        forward(src, c, False)
+
+    vlow[tokens:] = scatter_sum(gv_r, "rv_z").astype(BF)
+    back_all = nt(vlow[...], up[...]).astype(BF)
+    second = tn(first_proj, vlow[...]).astype(BF)
+
+    def adapter(at, carry):
+        z_at, c_at = at // 2, at % 2
+        ga[z_at, c_at, :, 0:shard] = tn(back_all, xv[:, columns(z_at, c_at)]).astype(BF)
+        ga[z_at, c_at, :, shard:] = second
+        return carry
+
+    lax.fori_loop(0, 2 * nz, adapter, 0)
+    scatter_pair(ga, ga_p, "ra_c")
+
+    forward(sources[last], c, False)
     for src in sources:
-        forward(src, c, False)
-    for src in [z] + sources:
         there = wfull.at[src, oc]
         rcopy(there, there, "w_c", src, src, partner).wait_recv()
         forward(src, oc, False)
-    first_proj = low[...].astype(BF)
     values = (acc[...] + adapter_scale * nn(first_proj, up[...])).astype(BF)
     vp[...] = values[tokens:]
     vloc[...] = values[:tokens]
     vall[z, c] = values[tokens:]
     gather_start(vp, vall, "v_z", "v_c")
-
-    vlow[tokens:] = scatter_sum(gv_r, "rv_z").astype(BF)
-    back_all = nt(vlow[...], up[...]).astype(BF)
-    second = tn(first_proj, vlow[...]).astype(BF)
-
-    def adapter(at, carry):
-        z_at, c_at = at // 2, at % 2
-        ga[z_at, c_at, :, 0:shard] = tn(back_all, xv[:, columns(z_at, c_at)]).astype(BF)
-        ga[z_at, c_at, :, shard:] = second
-        return carry
-
-    lax.fori_loop(0, 2 * nz, adapter, 0)
-    scatter_pair(ga, ga_p, "ra_c")
 
     def back(at, carry):
         z_at, c_at = at // 2, at % 2
@@ -344,36 +360,33 @@
         o_pg[:, columns(z_at, c_at)] = grad[tokens:]
         return carry
 
+    scatter_z(ga, ga_p, ga_h, ga_r, "ra_c", "ra_z")
     lax.fori_loop(0, nz, back, 0)
     gather_forward(vall, "v_z", "v_c")
-    scatter_z(ga, ga_p, ga_h, ga_r, "ra_c", "ra_z")
+    gg[g] = scatter_sum(ga_r, "ra_z").astype(BF)
+    for dg in range(1, n_group):
+        there = lax.rem(g + dg, n_group)
+        go(rcopy(gg.at[g], gg.at[g], "g", dg, n_group - dg, (there, j)))
     gather_finish(vall, "v_c")
 
     def key_head(head, carry):
         lanes = head_lanes(head)
         cs = stack(cv, head)
-        d_sel = nt(side(vall, lanes), masked(cs))
-        d_own = nt(vloc[:, lanes], jnp.concatenate(cs, axis=0))
-        p_sel = prob[head, 0:PROMPT_LEN]
-        p_own = prob[head, PROMPT_LEN:]
-        delta = jnp.sum(p_sel.astype(BF).astype(F32) * d_sel + p_own.astype(BF).astype(F32) * d_own,
-                        axis=0, keepdims=True)
-        g_sel = (p_sel * (d_sel - delta)).astype(BF)
-        g_own = (p_own * (d_own - delta)).astype(BF)
+        grad_full = nt(with_own(side(vall, lanes), vloc[:, lanes]), masked(cs))
+        full = prob[head]
+        delta = jnp.sum(full.astype(BF).astype(F32) * grad_full, axis=0, keepdims=True)
+        grad_low = (full * (grad_full - delta)).astype(BF)
         qs = stack(qv, head)
         per_half = KV_HEADS // 2
-        spread(gk.at[head // per_half], head_lanes(head % per_half), nn(g_sel, masked(qs)) * SCORE_SCALE)
-        o_rk[:, lanes] = (nn(g_own, jnp.concatenate(qs, axis=0)) * SCORE_SCALE).astype(BF)
+        grads = nn(grad_low, masked(qs)) * SCORE_SCALE
+        spread(gk.at[head // per_half], head_lanes(head % per_half), grads[:PROMPT_LEN])
+        o_rk[:, lanes] = own_sum(grads).astype(BF)
         return carry
 
     lax.fori_loop(0, KV_HEADS // 2, key_head, 0)
     scatter_pair(gk.at[0], gk_p.at[0], "rk_c")
     lax.fori_loop(KV_HEADS // 2, KV_HEADS - 1, key_head, 0)
     scatter_z(gk.at[0], gk_p.at[0], gk_h.at[0], gk_r.at[0], "rk_c", "rk_z")
-    gg[g] = scatter_sum(ga_r, "ra_z").astype(BF)
-    for dg in range(1, n_group):
-        there = lax.rem(g + dg, n_group)
-        go(rcopy(gg.at[g], gg.at[g], "g", dg, n_group - dg, (there, j)))
     lax.fori_loop(KV_HEADS - 1, KV_HEADS, key_head, 0)
     scatter_pair(gk.at[1], gk_p.at[1], "rk_c2")
     scatter_z(gk.at[1], gk_p.at[1], gk_h.at[1], gk_r.at[1], "rk_c2", "rk_z2")
@@ -455,7 +468,6 @@
             pltpu.VMEM((tokens, kv), BF),
             pltpu.VMEM((rows, kv), BF),
             pltpu.VMEM((tokens + rows, kv), F32),
-            pltpu.VMEM((tokens + rows, rank), F32),
             *reduce_space(rows, kv),
             *reduce_space(rows, kv // 2, (2,)),
             *reduce_space(rank, wide),

time: 63.9 us -> 66.1 us (1.034)
  Pallas kernels: 63.1 us -> 65.3 us
    pallas_call x1, Pallas kernels: 60.4 us -> 62.6 us  [on_device(): pl.pallas_call(functools.partial(kernel, nz, n_group, places, factor), ou...]
where the time goes in v5:
time: 66.1 us; the launch traced here: 65.9 us
  Pallas kernels  65.3 us (99%)
    pallas_call x1, Pallas kernels, on_device(): pl.pallas_call(functools.partial(kernel, nz, n_group, places, factor), ou...  62.6 us
    pallas_call x1, Pallas kernels, on_device(): pl.pallas_call(store, out_shape=tuple((jax.ShapeDtypeStruct(shape, kind)...  2.68 us

profile of v5, /device:TPU:0, one launch (start us, length us, event | category | flops | bytes accessed | tf_op | source)
XLA Modules:
  0.0 65.9 jit_solution(969408016878732675)
XLA Ops:
  0.6 62.6 %value_backward.1 = (bf16[128,4096]{1,0:T(8,128)(2,1)}, bf16[64,4096]{1,0:T(8,128)(2,1)}, bf16[128,512]{1,0:T(8,128)(2,1)}, bf16[64,512]{1,0:T(8,128)(2,1)}, f32[16,512]{1,0:T(8,128)}, /*index=5*/f32[16,512]{1,0:T(8,128)}) custom-call(bf16[128,4096]{1,0:T(8,128)(2,1)} %xr.1, bf16[64,4096]{1,0:T(8,128)(2,1)} %xp.1, bf16[128,4096]{1,0:T(8,128)(2,1)} %q.1, ...), custom_call_target="tpu_custom_call" | custom-call | tf_op jit(solution)/shard_map/value_backward/pallas_call | solution.py:451
  63.2 2.7 %store.1 = (bf16[128,4096]{1,0:T(8,128)(2,1)}, bf16[64,4096]{1,0:T(8,128)(2,1)}, bf16[128,512]{1,0:T(8,128)(2,1)}, bf16[64,512]{1,0:T(8,128)(2,1)}, f32[16,512]{1,0:T(8,128)}, /*index=5*/f32[16,512]{1,0:T(8,128)}) custom-call(bf16[128,4096]{1,0:T(8,128)(2,1)} %get-tuple-element.18.refs_0_, bf16[64,4096]{1,0:T(8,128)(2,1)} %get-tuple-element.19.refs_1_, ...), custom_call_target="tpu_custom_call" | custom-call | tf_op jit(solution)/shard_map/store/pallas_call | solution.py:486

commit v6 on v4

--- a/solution.py
+++ b/solution.py
@@ -61,7 +61,7 @@
     nz, n_group, places, factor,
     xr, xp, q, ct, w, rk, pk, seg, ch, dn, up,
     o_rg, o_pg, o_rk, o_pk, o_f, o_s,
-    xv, qv, cv, wfull, kall, vall, dall, pmask, obias, prob, vlow, vloc, vp, acc, low,
+    xv, qv, cv, wfull, kall, vall, dall, pmask, tmask, obias, prob, vlow, vloc, vp, acc, low,
     gv, gv_p, gv_h, gv_r, gk, gk_p, gk_h, gk_r, ga, ga_p, ga_h, ga_r, gg,
     ssem, rsem,
 ):
@@ -198,11 +198,12 @@
     token = lax.broadcasted_iota(jnp.int32, (tokens, tokens), 0)
     other = lax.broadcasted_iota(jnp.int32, (tokens, tokens), 1)
     obias[...] = jnp.where((seg_row == seg_col) & (token <= other), 0.0, -1e30)
-    choice = jnp.zeros((tokens, tokens), jnp.int32)
-    for at in range(ch.shape[1]):
-        choice = jnp.where(seg_col == float(at), ch[0, at], choice)
-    for at in range(prompts):
-        pmask[at] = jnp.where(choice == at, 1.0, 0.0).astype(BF)
+    for mask, segment in ((pmask, seg_col), (tmask, seg_row)):
+        choice = jnp.zeros((tokens, tokens), jnp.int32)
+        for at in range(ch.shape[1]):
+            choice = jnp.where(segment == float(at), ch[0, at], choice)
+        for at in range(prompts):
+            mask[at] = jnp.where(choice == at, 1.0, 0.0).astype(BF)
 
     def stack(ref, head):
         return [ref[:, pl.ds(pl.multiple_of((head * GROUP_SIZE + at) * HEAD_DIM, HEAD_DIM), HEAD_DIM)]
@@ -217,6 +218,20 @@
             [buf[at * nzp:(at + 1) * nzp, :, :, lanes].reshape(PROMPT_LEN, HEAD_DIM) for at in range(prompts)],
             axis=1)
 
+    def masked_turned(parts):
+        turned = [jnp.transpose(part) for part in parts]
+        return jnp.concatenate(
+            [jnp.concatenate([part * tmask[at] for part in turned], axis=1) for at in range(prompts)], axis=0)
+
+    def with_own(prompt_side, own):
+        return jnp.concatenate([prompt_side, jnp.concatenate([own] * prompts, axis=1)], axis=0)
+
+    def own_sum(grads):
+        total = grads[PROMPT_LEN:, 0:HEAD_DIM]
+        for at in range(1, prompts):
+            total = total + grads[PROMPT_LEN:, at * HEAD_DIM:(at + 1) * HEAD_DIM]
+        return total
+
     def head_lanes(head):
         return pl.ds(pl.multiple_of(head * HEAD_DIM, HEAD_DIM), HEAD_DIM)
 
@@ -228,9 +243,9 @@
     def softmax_head(head):
         lanes = head_lanes(head)
         qs = stack(qv, head)
-        s_sel = nt(side(kall, lanes), masked(qs)) * SCORE_SCALE
-        s_own = nt(rk[:, lanes], jnp.concatenate(qs, axis=0)) * SCORE_SCALE
-        s_own = s_own + jnp.concatenate([obias[...]] * GROUP_SIZE, axis=1)
+        scores = nn(with_own(side(kall, lanes), rk[:, lanes]), masked_turned(qs)) * SCORE_SCALE
+        s_sel = scores[:PROMPT_LEN]
+        s_own = scores[PROMPT_LEN:] + jnp.concatenate([obias[...]] * GROUP_SIZE, axis=1)
         top = jnp.max(jnp.maximum(s_sel, s_own), axis=0, keepdims=True)
         e_sel = jnp.exp(s_sel - top)
         e_own = jnp.exp(s_own - top)
@@ -240,8 +255,9 @@
         prob[head, 0:PROMPT_LEN] = p_sel
         prob[head, PROMPT_LEN:] = p_own
         cs = stack(cv, head)
-        spread(gv, lanes, nn(p_sel.astype(BF), masked(cs)))
-        vlow[0:tokens, lanes] = nn(p_own.astype(BF), jnp.concatenate(cs, axis=0)).astype(BF)
+        grads = nn(jnp.concatenate([p_sel.astype(BF), p_own.astype(BF)], axis=0), masked(cs))
+        spread(gv, lanes, grads[:PROMPT_LEN])
+        vlow[0:tokens, lanes] = own_sum(grads).astype(BF)
 
     def w_plane(src):
         there = wfull.at[src, c, mine]
@@ -352,18 +368,15 @@
     def key_head(head, carry):
         lanes = head_lanes(head)
         cs = stack(cv, head)
-        d_sel = nt(side(vall, lanes), masked(cs))
-        d_own = nt(vloc[:, lanes], jnp.concatenate(cs, axis=0))
-        p_sel = prob[head, 0:PROMPT_LEN]
-        p_own = prob[head, PROMPT_LEN:]
-        delta = jnp.sum(p_sel.astype(BF).astype(F32) * d_sel + p_own.astype(BF).astype(F32) * d_own,
-                        axis=0, keepdims=True)
-        g_sel = (p_sel * (d_sel - delta)).astype(BF)
-        g_own = (p_own * (d_own - delta)).astype(BF)
+        grad_full = nn(with_own(side(vall, lanes), vloc[:, lanes]), masked_turned(cs))
+        full = prob[head]
+        delta = jnp.sum(full.astype(BF).astype(F32) * grad_full, axis=0, keepdims=True)
+        grad_low = (full * (grad_full - delta)).astype(BF)
         qs = stack(qv, head)
         per_half = KV_HEADS // 2
-        spread(gk.at[head // per_half], head_lanes(head % per_half), nn(g_sel, masked(qs)) * SCORE_SCALE)
-        o_rk[:, lanes] = (nn(g_own, jnp.concatenate(qs, axis=0)) * SCORE_SCALE).astype(BF)
+        grads = nn(grad_low, masked(qs)) * SCORE_SCALE
+        spread(gk.at[head // per_half], head_lanes(head % per_half), grads[:PROMPT_LEN])
+        o_rk[:, lanes] = own_sum(grads).astype(BF)
         return carry
 
     lax.fori_loop(0, KV_HEADS // 2, key_head, 0)
@@ -449,6 +462,7 @@
             pltpu.VMEM((nz, 2, rows, kv), BF),
             pltpu.VMEM((nz, 2, rank, shard), BF),
             pltpu.VMEM((n_sample * rows // PROMPT_LEN, tokens, HEAD_DIM), BF),
+            pltpu.VMEM((n_sample * rows // PROMPT_LEN, HEAD_DIM, tokens), BF),
             pltpu.VMEM((tokens, tokens), F32),
             pltpu.VMEM((KV_HEADS, PROMPT_LEN + tokens, GROUP_SIZE * tokens), F32),
             pltpu.VMEM((tokens + rows, kv), BF),

time: 63.9 us -> 63.1 us (0.987)
  Pallas kernels: 63.1 us -> 62.3 us
    pallas_call x1, Pallas kernels: 60.4 us -> 59.6 us  [on_device(): pl.pallas_call(functools.partial(kernel, nz, n_group, places, factor), ou...]
where the time goes in v6:
time: 63.1 us; the launch traced here: 62.9 us
  Pallas kernels  62.3 us (99%)
  between operations  0.64 us (1%)
    pallas_call x1, Pallas kernels, on_device(): pl.pallas_call(functools.partial(kernel, nz, n_group, places, factor), ou...  59.6 us
    pallas_call x1, Pallas kernels, on_device(): pl.pallas_call(store, out_shape=tuple((jax.ShapeDtypeStruct(shape, kind)...  2.68 us

profile of v6, /device:TPU:0, one launch (start us, length us, event | category | flops | bytes accessed | tf_op | source)
XLA Modules:
  0.0 62.9 jit_solution(10806195339385802703)
XLA Ops:
  0.6 59.6 %value_backward.1 = (bf16[128,4096]{1,0:T(8,128)(2,1)}, bf16[64,4096]{1,0:T(8,128)(2,1)}, bf16[128,512]{1,0:T(8,128)(2,1)}, bf16[64,512]{1,0:T(8,128)(2,1)}, f32[16,512]{1,0:T(8,128)}, /*index=5*/f32[16,512]{1,0:T(8,128)}) custom-call(bf16[128,4096]{1,0:T(8,128)(2,1)} %xr.1, bf16[64,4096]{1,0:T(8,128)(2,1)} %xp.1, bf16[128,4096]{1,0:T(8,128)(2,1)} %q.1, ...), custom_call_target="tpu_custom_call" | custom-call | tf_op jit(solution)/shard_map/value_backward/pallas_call | solution.py:451
  60.3 2.7 %store.1 = (bf16[128,4096]{1,0:T(8,128)(2,1)}, bf16[64,4096]{1,0:T(8,128)(2,1)}, bf16[128,512]{1,0:T(8,128)(2,1)}, bf16[64,512]{1,0:T(8,128)(2,1)}, f32[16,512]{1,0:T(8,128)}, /*index=5*/f32[16,512]{1,0:T(8,128)}) custom-call(bf16[128,4096]{1,0:T(8,128)(2,1)} %get-tuple-element.18.refs_0_, bf16[64,4096]{1,0:T(8,128)(2,1)} %get-tuple-element.19.refs_1_, ...), custom_call_target="tpu_custom_call" | custom-call | tf_op jit(solution)/shard_map/store/pallas_call | solution.py:488
